TPU v7x, 128 devices: a whole 4x4x4 slice. The times are simulated.
128 devices in a mesh: gx: 8 (over y, core), gy: 16 (over z, x).
Axes of the slice: x: 4, y: 4, z: 4, core: 2. Of those that a mesh axis runs over, the one named last changes fastest.
Arguments:
- fluid_temp: float32 [256, 512, 512], P('gx', 'gy'), may hold values from -6 to 6
- kappa: bfloat16 [256, 512, 512], P('gx', 'gy'), may hold values from 0.019897461 to 0.13964844
- velocity: bfloat16 [3, 256, 512, 512], P(None, 'gx', 'gy'), may hold values from -0.19921875 to 0.19921875
- wall_temp: float32 [256, 512], P('gx', 'gy'), may hold values from -6 to 6
- face_count: int32 [128], P(('gx', 'gy')), may hold values from 1 to 8, 256 in all
- face_map: int32 [256], replicated, may hold values from 0 to 255, each once
- solid_temp: float32 [256, 32, 128], P(('gx', 'gy')), may hold values from -6 to 6
- solid_cond: float32 [256, 32, 128], P(('gx', 'gy')), may hold values from 0.5 to 2
- coolant: float32 [256, 128], P(('gx', 'gy')), may hold values from -6 to 6
Outputs:
- fluid_out: float32 [256, 512, 512], P('gx', 'gy')
- wall_out: float32 [256, 512], P('gx', 'gy')
- solid_out: float32 [256, 32, 128], P(('gx', 'gy'))
Inputs may be any that keep to these rules, and one draw needn't show every extreme that they name: Each fluid device's first face_count face blocks are active; the counts add up to 256 and one device has exactly 8. `face_map`: A permutation: every solid face block is coupled to exactly one active fluid face block.
All inputs are finite; a program needn't handle non-finite values.
Results may differ from a plain program's by a relative error of at most 0.0014.
Values may be sent and summed in bfloat16 or wider, within the bound.
A program may use at most 128 MiB of HBM per device.

v0:
```python
import jax
import jax.numpy as jnp
from jax import lax
from jax.sharding import PartitionSpec as P

FACE = 128
SWEEPS = 6


wall_ratio = 25.0
cool_coef = 1.0


def with_halo(block, sides, width):
    for axis, dim in sides:
        count = lax.axis_size(axis)
        forward = [(i, i + 1) for i in range(count - 1)]
        backward = [(target, source) for source, target in forward]
        low = lax.ppermute(
            lax.slice_in_dim(block, block.shape[dim] - width, None, axis=dim), axis, forward
        )
        high = lax.ppermute(lax.slice_in_dim(block, 0, width, axis=dim), axis, backward)
        block = jnp.concatenate([low, block, high], axis=dim)
    return block


def entering(array, axis, combine, identity):
    count, place = (lax.axis_size(axis), lax.axis_index(axis))
    everything = lax.all_gather(array, axis)
    start = jnp.broadcast_to(jnp.asarray(identity, array.dtype), array.shape)

    def turn(k, before):
        reached = k < place
        new = combine(before, everything[k])
        return jnp.where(reached, new, before)

    return lax.fori_loop(0, count, turn, start)


def face_term(center, cond_mid, neighbor, cond_nb, flow_nb, flow_mid, orient):
    face_cond = 0.5 * (cond_mid + cond_nb)
    face_flow = 0.5 * (flow_mid + flow_nb)
    return face_cond * (neighbor - center) - orient * face_flow * 0.5 * (center + neighbor)


def advance(padded, wall_plane, cond_pad, flow_x, flow_y, flow_z):
    center = padded[1:-1, 1:-1]
    cond_mid = cond_pad[1:-1, 1:-1].astype(jnp.float32)
    mid_x = flow_x[1:-1, 1:-1].astype(jnp.float32)
    mid_y = flow_y[1:-1, 1:-1].astype(jnp.float32)
    mid_z = flow_z.astype(jnp.float32)
    updated = center + face_term(
        center,
        cond_mid,
        padded[2:, 1:-1],
        cond_pad[2:, 1:-1].astype(jnp.float32),
        flow_x[2:, 1:-1].astype(jnp.float32),
        mid_x,
        1.0,
    )
    updated = updated + face_term(
        center,
        cond_mid,
        padded[:-2, 1:-1],
        cond_pad[:-2, 1:-1].astype(jnp.float32),
        flow_x[:-2, 1:-1].astype(jnp.float32),
        mid_x,
        -1.0,
    )
    updated = updated + face_term(
        center,
        cond_mid,
        padded[1:-1, 2:],
        cond_pad[1:-1, 2:].astype(jnp.float32),
        flow_y[1:-1, 2:].astype(jnp.float32),
        mid_y,
        1.0,
    )
    updated = updated + face_term(
        center,
        cond_mid,
        padded[1:-1, :-2],
        cond_pad[1:-1, :-2].astype(jnp.float32),
        flow_y[1:-1, :-2].astype(jnp.float32),
        mid_y,
        -1.0,
    )
    zero_col = jnp.zeros_like(center[..., :1])
    upper = jnp.concatenate([center[..., 1:], zero_col], axis=-1)
    lower = jnp.concatenate([wall_plane[..., None], center[..., :-1]], axis=-1)
    cond_up = jnp.concatenate([cond_mid[..., 1:], zero_col], axis=-1)
    cond_down = jnp.concatenate([zero_col, cond_mid[..., :-1]], axis=-1)
    flow_up = jnp.concatenate([mid_z[..., 1:], zero_col], axis=-1)
    flow_down = jnp.concatenate([zero_col, mid_z[..., :-1]], axis=-1)
    updated = updated + face_term(center, cond_mid, upper, cond_up, flow_up, mid_z, 1.0)
    updated = updated + face_term(center, cond_mid, lower, cond_down, flow_down, mid_z, -1.0)
    return updated


def sweeps(temps, conds, near_wall, wall_cond, coolant):
    nblk, layers, width = temps.shape
    heat_wall = wall_ratio * wall_cond
    depth_cond = 0.5 * (conds[:, 1:] + conds[:, :-1])
    side_cond = 0.5 * (conds[:, :, 1:] + conds[:, :, :-1])
    zero_layer = jnp.zeros((nblk, 1, width), jnp.float32)
    zero_side = jnp.zeros((nblk, layers, 1), jnp.float32)
    middle = jnp.zeros((nblk, layers - 2, width), jnp.float32)
    cond_up = jnp.concatenate([zero_layer, depth_cond], axis=1)
    cond_down = jnp.concatenate([depth_cond, zero_layer], axis=1)
    cond_left = jnp.concatenate([zero_side, side_cond], axis=2)
    cond_right = jnp.concatenate([side_cond, zero_side], axis=2)
    bound_coef = jnp.concatenate(
        [heat_wall[:, None, :], middle, jnp.full((nblk, 1, width), cool_coef, jnp.float32)], axis=1
    )
    source = jnp.concatenate(
        [(heat_wall * near_wall)[:, None, :], middle, (cool_coef * coolant)[:, None, :]], axis=1
    )
    denom = cond_up + cond_down + cond_left + cond_right + bound_coef
    for repeat in range(SWEEPS):
        neighbors = cond_up * jnp.concatenate([zero_layer, temps[:, :-1]], axis=1)
        neighbors = neighbors + cond_down * jnp.concatenate([temps[:, 1:], zero_layer], axis=1)
        neighbors = neighbors + cond_left * jnp.concatenate([zero_side, temps[:, :, :-1]], axis=2)
        neighbors = neighbors + cond_right * jnp.concatenate([temps[:, :, 1:], zero_side], axis=2)
        temps = (neighbors + source) / denom
    return temps


def accumulate(earlier, later):
    return earlier + later


def shards(
    fluid_temp, kappa, velocity, wall_temp, face_count, face_map, solid_temp, solid_cond, coolant
):
    plane_x, plane_y = wall_temp.shape
    static = jnp.stack([kappa, velocity[0], velocity[1]])
    static_pad = with_halo(static, (("gx", 1), ("gy", 2)), 1)

    def one_step(field):
        padded = with_halo(field, (("gx", 0), ("gy", 1)), 1)
        return advance(padded, wall_temp, static_pad[0], static_pad[1], static_pad[2], velocity[2])

    fluid_out = one_step(one_step(fluid_temp))
    width = FACE
    blocks = plane_x * plane_y // width
    solid_rows = solid_temp.shape[0]
    total_solid = face_map.shape[0]
    position = lax.axis_index(("gx", "gy"))
    my_count = face_count[0]
    start_rank = entering(face_count, ("gx", "gy"), accumulate, jnp.zeros_like(face_count))[0]
    slots = jnp.arange(blocks, dtype=jnp.int32)
    active = slots < my_count
    ranks = jnp.minimum(start_rank + slots, total_solid - 1)
    targets = jnp.where(active, jnp.take(face_map, ranks), -1)
    near_wall = fluid_out[:, :, 0].reshape(blocks, width)
    wall_cond = (0.5 * kappa[:, :, 0].astype(jnp.float32)).reshape(blocks, width)
    payload = jnp.stack([near_wall, wall_cond], axis=1)
    owned = (position * solid_rows + jnp.arange(solid_rows, dtype=jnp.int32)).astype(jnp.float32)
    loads = lax.all_gather(payload, ("gx", "gy"), axis=0, tiled=True)
    labels = lax.all_gather(targets.astype(jnp.float32), ("gx", "gy"), axis=0, tiled=True)
    picker = (labels[None, :] == owned[:, None]).astype(jnp.float32)
    incoming = jnp.einsum("sk,kcf->scf", picker, loads, precision=lax.Precision.HIGHEST)
    solid_out = sweeps(solid_temp, solid_cond, incoming[:, 0], incoming[:, 1], coolant)
    surface = solid_out[:, 0, :]
    piece = lax.all_gather(surface, ("gx", "gy"), axis=0, tiled=True)
    piece_rows = piece.shape[0]
    picker = (targets[:, None] == jnp.arange(piece_rows, dtype=jnp.int32)[None, :]).astype(
        jnp.float32
    )
    returned = jnp.dot(picker, piece, precision=lax.Precision.HIGHEST)
    wall_blocks = jnp.where(active[:, None], returned, wall_temp.reshape(blocks, width))
    return (fluid_out, wall_blocks.reshape(plane_x, plane_y), solid_out)


def solution(mesh):
    return jax.shard_map(
        shards,
        mesh=mesh,
        in_specs=(
            P("gx", "gy", None),
            P("gx", "gy", None),
            P(None, "gx", "gy", None),
            P("gx", "gy"),
            P(("gx", "gy")),
            P(),
            P(("gx", "gy"), None, None),
            P(("gx", "gy"), None, None),
            P(("gx", "gy"), None),
        ),
        out_specs=(P("gx", "gy", None), P("gx", "gy"), P(("gx", "gy"), None, None)),
        check_vma=False,
    )
```

profile of v0, /device:TPU:1, one launch (start us, length us, event | category | flops | bytes accessed | tf_op | source)
XLA Modules:
  0.0 451.3 jit_solution(8742725063439301551)
XLA Ops:
  7.2 1.5 slice-done
  8.8 1.2 copy.47
  10.0 0.6 copy.65
  10.6 1.0 pad_maximum_fusion.20
  11.6 4.8 %collective-permute-start = (bf16[3,1,32,512]{3,1,2,0:T(2,128)(2,1)}, bf16[3,1,32,512]{3,1,2,0:T(2,128)(2,1)S(1)}, u32[]{:S(2)}, u32[]{:S(2)}) collective-permute-start(bf16[3,1,32,512]{3,1,2,0:T(2,128)(2,1)} %get-tuple-element.101), channel_id=1, source_target_pairs={{0,16},{16,32},{32,48},{48,64},{64,80},{80,96},{96,112},{1,17},{17... | collective-permute-start | bytes 294920 | tf_op jit(solution)/shard_map/ppermute | solution.py:19
  16.5 1.9 collective-permute-start.1
  18.5 0.7 copy.20
  19.1 1.9 collective-permute-start.4
  21.1 0.7 copy.25
  21.7 3.6 collective-permute-start.5
  25.5 1.2 copy.24
  26.7 0.6 fusion.62
  27.4 4.8 %fusion.86 = (f32[32,32,511]{2,0,1:T(8,128)}, f32[32,32,511]{2,0,1:T(8,128)}, f32[32,32,511]{2,0,1:T(8,128)}, f32[32,32,511]{2,0,1:T(8,128)}) fusion(f32[32,32,512]{2,0,1:T(8,128)S(1)} %fusion.62, f32[32,32,512]{2,0,1:T(8,128)S(1)} %copy.24), kind=kLoop, calls=%fused_computation.154 | loop fusion | bytes 16744448 | tf_op jit(solution)/shard_map/slice | solution.py:94
  32.1 2.0 copy.39
  34.1 1.0 pad_maximum_fusion.24
  35.1 3.3 collective-permute-start.2
  38.3 1.3 collective-permute-start.3
  39.6 0.7 pad_maximum_fusion.30
  40.4 1.3 collective-permute-start.6
  41.7 4.8 %collective-permute-start.7 = (f32[34,1,512]{2,0,1:T(8,128)S(1)}, f32[34,1,512]{2,0,1:T(8,128)S(1)}, u32[]{:S(2)}, u32[]{:S(2)}) collective-permute-start(f32[34,1,512]{2,0,1:T(8,128)S(1)} %get-tuple-element.106), channel_id=1, source_target_pairs={{0,1},{1,2},{2,3},{3,4},{4,5},{5,6},{6,7},{7,8},{8,9},{9,10},{10,1... | collective-permute-start | bytes 208904 | tf_op jit(solution)/shard_map/ppermute | solution.py:19
  46.5 2.8 pad_maximum_fusion
  50.0 0.8 fusion.87
  51.1 1.7 copy-done.21
  52.9 1.5 copy-done.22
  54.4 0.6 copy-done.2
  55.0 0.6 copy-done.13
  55.6 0.6 copy-done.15
  56.4 11.4 %fusion.42 = f32[32,32,512]{2,0,1:T(8,128)S(1)} fusion(f32[32,32,512]{2,0,1:T(8,128)S(1)} %copy-done.2, f32[1,32,512]{2,0,1:T(1,128)} %collective-permute-done.4, f32[1,32,512]{2,0,1:T(1,128)} %collective-permute-done.5, f32[34,1,512]{2,0,1:T(8,128)S(1)} %collective-permute-done.7, f32[34,1,512]{2,0,1:T(8,128)S(1)} %collective-permute-done.6, ...), kind=kLoop, calls=%fused_computation.68 | loop fusion | flops 42467328 | bytes 29609984 | tf_op jit(solution)/shard_map/add | solution.py:96
  67.8 0.8 fusion.85
  68.5 2.1 collective-permute-start.8
  70.7 3.4 collective-permute-start.9
  74.1 1.2 multiply_reduce_fusion
  75.7 0.9 pad_maximum_fusion.27
  76.6 1.3 collective-permute-start.10
  77.9 4.3 collective-permute-start.11
  82.2 0.7 fusion.84
  83.0 1.5 collective-permute-done.11
  84.5 11.7 %fusion.16 = f32[32,32,512]{2,0,1:T(8,128)S(1)} fusion(f32[32,32,512]{2,0,1:T(8,128)S(1)} %fusion.42, f32[1,32,512]{2,0,1:T(1,128)} %collective-permute-done.8, f32[1,32,512]{2,0,1:T(1,128)} %collective-permute-done.9, f32[34,1,512]{2,0,1:T(8,128)S(1)} %collective-permute-done.11, f32[34,1,512]{2,0,1:T(8,128)S(1)} %collective-permute-done.10, ...), kind=kLoop, calls=%fused_computation.34 | loop fusion | flops 42467328 | bytes 29609984 | tf_op jit(solution)/shard_map/add | solution.py:96
  96.2 1.3 copy-done.19
  98.1 0.6 pad_maximum_fusion.32
  99.8 74.8 %all-reduce.34 = s32[128]{0:T(128)S(1)} all-reduce(s32[128]{0:T(128)S(1)} %dynamic-update-slice), channel_id=2, replica_groups=mesh['gx'=8,'gy'=16] {'gx','gy'}, use_global_device_ids=true, to_apply=%add.34 | all-reduce | flops 128 | bytes 1024
  174.5 148.5 %while.13 = (s32[]{:T(128)}, s32[1]{0:T(128)}, s32[]{:T(128)}, s32[128,1]{0,1:T(1,128)S(1)}, s32[]{:T(128)}) while((s32[]{:T(128)}, s32[1]{0:T(128)}, s32[]{:T(128)}, s32[128,1]{0,1:T(1,128)S(1)}, s32[]{:T(128)}) %tuple.66), condition=%wide.region_1.2_spmd, body=%wide.region_0.1_spmd.sunk | while | flops 5 | bytes 107 | solution.py:37
  323.1 0.6 gather_fusion
  323.9 62.8 %all-reduce.35 = f32[1024]{0:T(1024)S(1)} all-reduce(f32[1024]{0:T(1024)S(1)} %get-tuple-element.94), channel_id=1, replica_groups=mesh['gx'=8,'gy'=16] {'gx','gy'}, use_global_device_ids=true, to_apply=%add.35 | all-reduce | flops 1024 | bytes 8192
  386.9 4.1 copy.46
  391.1 1.7 fusion.75
  393.9 49.7 %all-gather.1 = f32[256,1,128]{2,1,0:T(1,128)S(1)} all-gather(f32[2,1,128]{2,1,0:T(1,128)S(1)} %slice.386), channel_id=3, replica_groups=mesh['gx'=8,'gy'=16] {'gx','gy'}, dimensions={0}, use_global_device_ids=true | all-gather | bytes 132096 | tf_op jit(solution)/shard_map/all_gather | solution.py:165
  443.8 0.7 reshape.78
  (244 shorter events, 78.2 us)
Async XLA Ops:
  7.2 315.9 %copy-start = (s32[256]{0:T(256)S(1)}, s32[256]{0:T(256)}, u32[]{:S(2)}) copy-start(s32[256]{0:T(256)} %param.16) | copy-start | bytes 3076
  7.2 1.6 slice-start
  7.2 383.9 %all-gather.4.cloned.1.call-start = ((), (), s32[]{:S(2)}) async-start(), calls=%async_computation | async-start | bytes 1056768 | tf_op jit(solution)/shard_map/all_gather | solution.py:159
  8.8 1.2 copy-start.26
  10.0 1.6 copy-start.7
  10.0 8.4 %copy-start.25 = (f32[32,32,512]{2,1,0:T(8,128)S(1)}, f32[32,32,512]{2,1,0:T(8,128)}, u32[]{:S(2)}) copy-start(f32[32,32,512]{2,1,0:T(8,128)} %param.11) | copy-start | bytes 6291460
  10.6 14.8 %copy-start.20 = (bf16[3,32,32,512]{3,2,1,0:T(8,128)(2,1)S(1)}, bf16[3,32,32,512]{3,2,1,0:T(8,128)(2,1)}, u32[]{:S(2)}) copy-start(bf16[3,32,32,512]{3,2,1,0:T(8,128)(2,1)} %param.13) | copy-start | bytes 9437188
  11.6 22.4 %collective-permute-start = (bf16[3,1,32,512]{3,1,2,0:T(2,128)(2,1)}, bf16[3,1,32,512]{3,1,2,0:T(2,128)(2,1)S(1)}, u32[]{:S(2)}, u32[]{:S(2)}) collective-permute-start(bf16[3,1,32,512]{3,1,2,0:T(2,128)(2,1)} %get-tuple-element.101), channel_id=1, source_target_pairs={{0,16},{16,32},{32,48},{48,64},{64,80},{80,96},{96,112},{1,17},{17... | collective-permute-start | bytes 294920 | tf_op jit(solution)/shard_map/ppermute | solution.py:19
  16.5 17.6 %collective-permute-start.1 = (bf16[3,1,32,512]{3,1,2,0:T(2,128)(2,1)}, bf16[3,1,32,512]{3,1,2,0:T(2,128)(2,1)S(1)}, u32[]{:S(2)}, u32[]{:S(2)}) collective-permute-start(bf16[3,1,32,512]{3,1,2,0:T(2,128)(2,1)} %get-tuple-element.102), channel_id=1, source_target_pairs={{16,0},{32,16},{48,32},{64,48},{80,64},{96,80},{112,96},{17,1},{33... | collective-permute-start | bytes 294920 | tf_op jit(solution)/shard_map/ppermute | solution.py:22
  19.1 20.5 %collective-permute-start.4 = (f32[1,32,512]{2,0,1:T(1,128)}, f32[1,32,512]{2,0,1:T(1,128)}, u32[]{:S(2)}, u32[]{:S(2)}) collective-permute-start(f32[1,32,512]{2,0,1:T(1,128)} %copy.20), channel_id=1, source_target_pairs={{16,0},{32,16},{48,32},{64,48},{80,64},{96,80},{112,96},{17,1},{33... | collective-permute-start | bytes 196616 | tf_op jit(solution)/shard_map/ppermute | solution.py:22
  21.7 17.9 %collective-permute-start.5 = (f32[1,32,512]{2,0,1:T(1,128)}, f32[1,32,512]{2,0,1:T(1,128)}, u32[]{:S(2)}, u32[]{:S(2)}) collective-permute-start(f32[1,32,512]{2,0,1:T(1,128)} %copy.25), channel_id=1, source_target_pairs={{0,16},{16,32},{32,48},{48,64},{64,80},{80,96},{96,112},{1,17},{17... | collective-permute-start | bytes 196616 | tf_op jit(solution)/shard_map/ppermute | solution.py:19
  25.5 1.9 copy-start.16
  26.7 12.9 %copy-start.1 = (f32[32,32,512]{2,0,1:T(8,128)}, f32[32,32,512]{2,0,1:T(8,128)S(1)}, u32[]{:S(2)}) copy-start(f32[32,32,512]{2,0,1:T(8,128)S(1)} %copy.24) | copy-start | bytes 6291460
  35.0 11.5 %copy-start.8 = (bf16[2,32,32,512]{3,1,2,0:T(8,128)(2,1)S(1)}, bf16[2,32,32,512]{3,1,2,0:T(8,128)(2,1)}, u32[]{:S(2)}) copy-start(bf16[2,32,32,512]{3,1,2,0:T(8,128)(2,1)} %copy-done.7) | copy-start | bytes 6291460
  35.1 11.4 %collective-permute-start.2 = (bf16[3,34,1,512]{3,1,2,0:T(8,128)(2,1)S(1)}, bf16[3,34,1,512]{3,1,2,0:T(8,128)(2,1)S(1)}, u32[]{:S(2)}, u32[]{:S(2)}) collective-permute-start(bf16[3,34,1,512]{3,1,2,0:T(8,128)(2,1)S(1)} %get-tuple-element.99), channel_id=1, source_target_pairs={{0,1},{1,2},{2,3},{3,4},{4,5},{5,6},{6,7},{7,8},{8,9},{9,10},{10,1... | collective-permute-start | bytes 313352 | tf_op jit(solution)/shard_map/ppermute | solution.py:19
  38.3 8.2 %collective-permute-start.3 = (bf16[3,34,1,512]{3,1,2,0:T(8,128)(2,1)S(1)}, bf16[3,34,1,512]{3,1,2,0:T(8,128)(2,1)S(1)}, u32[]{:S(2)}, u32[]{:S(2)}) collective-permute-start(bf16[3,34,1,512]{3,1,2,0:T(8,128)(2,1)S(1)} %get-tuple-element.100), channel_id=1, source_target_pairs={{1,0},{2,1},{3,2},{4,3},{5,4},{6,5},{7,6},{8,7},{9,8},{10,9},{11,1... | collective-permute-start | bytes 313352 | tf_op jit(solution)/shard_map/ppermute | solution.py:22
  40.4 10.4 %collective-permute-start.6 = (f32[34,1,512]{2,0,1:T(8,128)S(1)}, f32[34,1,512]{2,0,1:T(8,128)S(1)}, u32[]{:S(2)}, u32[]{:S(2)}) collective-permute-start(f32[34,1,512]{2,0,1:T(8,128)S(1)} %get-tuple-element.105), channel_id=1, source_target_pairs={{1,0},{2,1},{3,2},{4,3},{5,4},{6,5},{7,6},{8,7},{9,8},{10,9},{11,1... | collective-permute-start | bytes 208904 | tf_op jit(solution)/shard_map/ppermute | solution.py:22
  41.7 9.1 %collective-permute-start.7 = (f32[34,1,512]{2,0,1:T(8,128)S(1)}, f32[34,1,512]{2,0,1:T(8,128)S(1)}, u32[]{:S(2)}, u32[]{:S(2)}) collective-permute-start(f32[34,1,512]{2,0,1:T(8,128)S(1)} %get-tuple-element.106), channel_id=1, source_target_pairs={{0,1},{1,2},{2,3},{3,4},{4,5},{5,6},{6,7},{7,8},{8,9},{9,10},{10,1... | collective-permute-start | bytes 208904 | tf_op jit(solution)/shard_map/ppermute | solution.py:19
  49.3 1.8 copy-start.23
  49.6 1.2 copy-start.3
  49.6 1.5 copy-start.5
  49.6 3.2 copy-start.21
  49.6 4.7 %copy-start.22 = (f32[32,32,511]{2,0,1:T(8,128)S(1)}, f32[32,32,511]{2,0,1:T(8,128)}, u32[]{:S(2)}) copy-start(f32[32,32,511]{2,0,1:T(8,128)} %get-tuple-element.146) | copy-start | bytes 6279172
  50.0 5.0 %copy-start.2 = (f32[32,32,512]{2,0,1:T(8,128)S(1)}, f32[32,32,512]{2,0,1:T(8,128)}, u32[]{:S(2)}) copy-start(f32[32,32,512]{2,0,1:T(8,128)} %copy-done.1) | copy-start | bytes 6291460
  50.0 5.6 %copy-start.13 = (f32[32,32,511]{2,0,1:T(8,128)S(1)}, f32[32,32,511]{2,0,1:T(8,128)}, u32[]{:S(2)}) copy-start(f32[32,32,511]{2,0,1:T(8,128)} %get-tuple-element.111) | copy-start | bytes 6279172
  50.0 6.2 %copy-start.15 = (f32[32,32,511]{2,0,1:T(8,128)S(1)}, f32[32,32,511]{2,0,1:T(8,128)}, u32[]{:S(2)}) copy-start(f32[32,32,511]{2,0,1:T(8,128)} %get-tuple-element.112) | copy-start | bytes 6279172
  50.0 6.4 %copy-start.17 = (bf16[1,32,32,512]{3,2,1,0:T(8,128)(2,1)S(1)}, bf16[1,32,32,512]{3,2,1,0:T(8,128)(2,1)}, u32[]{:S(2)}) copy-start(bf16[1,32,32,512]{3,2,1,0:T(8,128)(2,1)} %copy-done.16) | copy-start | bytes 3145732
  50.8 17.0 %copy-start.9 = (f32[32,32,511]{2,0,1:T(8,128)}, f32[32,32,511]{2,0,1:T(8,128)S(1)}, u32[]{:S(2)}) copy-start(f32[32,32,511]{2,0,1:T(8,128)S(1)} %get-tuple-element.113) | copy-start | bytes 6279172
  50.8 17.0 %copy-start.11 = (f32[32,32,511]{2,0,1:T(8,128)}, f32[32,32,511]{2,0,1:T(8,128)S(1)}, u32[]{:S(2)}) copy-start(f32[32,32,511]{2,0,1:T(8,128)S(1)} %get-tuple-element.114) | copy-start | bytes 6279172
  68.5 6.8 %collective-permute-start.8 = (f32[1,32,512]{2,0,1:T(1,128)}, f32[1,32,512]{2,0,1:T(1,128)}, u32[]{:S(2)}, u32[]{:S(2)}) collective-permute-start(f32[1,32,512]{2,0,1:T(1,128)} %get-tuple-element.110), channel_id=1, source_target_pairs={{16,0},{32,16},{48,32},{64,48},{80,64},{96,80},{112,96},{17,1},{33... | collective-permute-start | bytes 196616 | tf_op jit(solution)/shard_map/ppermute | solution.py:22
  70.7 5.1 %collective-permute-start.9 = (f32[1,32,512]{2,0,1:T(1,128)}, f32[1,32,512]{2,0,1:T(1,128)}, u32[]{:S(2)}, u32[]{:S(2)}) collective-permute-start(f32[1,32,512]{2,0,1:T(1,128)} %get-tuple-element.109), channel_id=1, source_target_pairs={{0,16},{16,32},{32,48},{48,64},{64,80},{80,96},{96,112},{1,17},{17... | collective-permute-start | bytes 196616 | tf_op jit(solution)/shard_map/ppermute | solution.py:19
  75.7 8.7 %copy-start.14 = (f32[32,32,511]{2,0,1:T(8,128)S(1)}, f32[32,32,511]{2,0,1:T(8,128)}, u32[]{:S(2)}) copy-start(f32[32,32,511]{2,0,1:T(8,128)} %get-tuple-element.111) | copy-start | bytes 6279172
  75.7 8.7 %copy-start.24 = (f32[32,32,1]{2,0,1:T(8,128)S(1)}, f32[32,32,1]{2,0,1:T(8,128)}, u32[]{:S(2)}) copy-start(f32[32,32,1]{2,0,1:T(8,128)} %copy.39) | copy-start | bytes 12292
  76.6 6.3 %collective-permute-start.10 = (f32[34,1,512]{2,0,1:T(8,128)S(1)}, f32[34,1,512]{2,0,1:T(8,128)S(1)}, u32[]{:S(2)}, u32[]{:S(2)}) collective-permute-start(f32[34,1,512]{2,0,1:T(8,128)S(1)} %get-tuple-element.103), channel_id=1, source_target_pairs={{1,0},{2,1},{3,2},{4,3},{5,4},{6,5},{7,6},{8,7},{9,8},{10,9},{11,1... | collective-permute-start | bytes 208904 | tf_op jit(solution)/shard_map/ppermute | solution.py:22
  77.9 6.5 %copy-start.10 = (f32[32,32,511]{2,0,1:T(8,128)S(1)}, f32[32,32,511]{2,0,1:T(8,128)}, u32[]{:S(2)}) copy-start(f32[32,32,511]{2,0,1:T(8,128)} %copy-done.9) | copy-start | bytes 6279172
  77.9 6.5 %copy-start.12 = (f32[32,32,511]{2,0,1:T(8,128)S(1)}, f32[32,32,511]{2,0,1:T(8,128)}, u32[]{:S(2)}) copy-start(f32[32,32,511]{2,0,1:T(8,128)} %copy-done.11) | copy-start | bytes 6279172
  77.9 6.5 %copy-start.18 = (bf16[1,32,32,512]{3,2,1,0:T(8,128)(2,1)S(1)}, bf16[1,32,32,512]{3,2,1,0:T(8,128)(2,1)}, u32[]{:S(2)}) copy-start(bf16[1,32,32,512]{3,2,1,0:T(8,128)(2,1)} %copy-done.16) | copy-start | bytes 3145732
  77.9 6.5 %collective-permute-start.11 = (f32[34,1,512]{2,0,1:T(8,128)S(1)}, f32[34,1,512]{2,0,1:T(8,128)S(1)}, u32[]{:S(2)}, u32[]{:S(2)}) collective-permute-start(f32[34,1,512]{2,0,1:T(8,128)S(1)} %get-tuple-element.104), channel_id=1, source_target_pairs={{0,1},{1,2},{2,3},{3,4},{4,5},{5,6},{6,7},{7,8},{8,9},{9,10},{10,1... | collective-permute-start | bytes 208904 | tf_op jit(solution)/shard_map/ppermute | solution.py:19
  82.2 2.3 copy-start.4
  82.2 2.3 copy-start.6
  84.5 14.3 %copy-start.29 = (f32[32,32]{1,0:T(8,128)S(1)}, f32[32,32]{1,0:T(8,128)}, u32[]{:S(2)}) copy-start(f32[32,32]{1,0:T(8,128)} %param.14) | copy-start | bytes 12292
  96.2 1.3 copy-start.19
  97.6 289.1 %copy-start.27 = (f32[2,32,128]{2,1,0:T(8,128)S(1)}, f32[2,32,128]{2,1,0:T(8,128)}, u32[]{:S(2)}) copy-start(f32[2,32,128]{2,1,0:T(8,128)} %param.18) | copy-start | bytes 98308
  97.6 289.2 %copy-start.28 = (f32[2,32,128]{2,1,0:T(8,128)S(1)}, f32[2,32,128]{2,1,0:T(8,128)}, u32[]{:S(2)}) copy-start(f32[2,32,128]{2,1,0:T(8,128)} %param.17) | copy-start | bytes 98308
  386.9 5.8 %copy-start.30 = (f32[2,128]{1,0:T(2,128)S(1)}, f32[2,128]{1,0:T(2,128)}, u32[]{:S(2)}) copy-start(f32[2,128]{1,0:T(2,128)} %param.19) | copy-start | bytes 3076
  393.9 50.6 %copy-start.31 = (f32[2,32,128]{2,1,0:T(8,128)}, f32[2,32,128]{2,1,0:T(8,128)S(1)}, u32[]{:S(2)}) copy-start(f32[2,32,128]{2,1,0:T(8,128)S(1)} %fusion.74) | copy-start | bytes 98308
Sparse Core Ops, SparseCore 0:
  98.9 72.6 all-gather.3
where the time goes:
time: 453 us; the launch traced here: 451 us
  blocking collectives  187 us (41%)
  local copies, waits for them, and re-layouts  103 us (23%)
  loops' own time  74.6 us (16%)
  starting transfers between devices  34.1 us (8%)
  other arithmetic  33 us (7%)
  between operations  15.4 us (3%)
    unnamed x2, blocking collectives  138 us
    another operation x1, loops' own time, entering(): return lax.fori_loop(0, count, turn, start)  74.6 us
    dynamic_slice x128, local copies, waits for them, and re-layouts, turn(): new = combine(before, everything[k])  73.9 us
    all_gather x1, blocking collectives, shards(): piece = lax.all_gather(surface, ('gx', 'gy'), axis=0, tiled=True)  49.7 us
    ppermute x6, starting transfers between devices, with_halo(): lax.ppermute(lax.slice_in_dim(block, block.shape[dim] - width, None, axis...  24.2 us
    add x2, other arithmetic, advance(): updated + face_term(center, cond_mid, lower, cond_down, flow_down, mid_z,...  23.1 us
    unnamed x71, local copies, waits for them, and re-layouts  14.3 us
    ppermute x6, starting transfers between devices, with_halo(): lax.ppermute(lax.slice_in_dim(block, 0, width, axis=dim), axis, backward)  9.81 us
  transfers between devices with their start and end apart: 13, of which 2 were waited for; matrix products, arithmetic and copies ran while one was open for 22% of the time, Pallas kernels for 0%

commit v1 on v0

v1 whole, which is shorter than its diff:
```python
import functools

import jax
import jax.numpy as jnp
from jax import lax
from jax.experimental import pallas as pl
from jax.experimental.pallas import tpu as pltpu
from jax.sharding import PartitionSpec as P

MESH = pl.DeviceIdType.MESH
F32 = jnp.float32
SWEEPS = 6
WALL_RATIO = 25.0
COOL = 1.0
EXACT = lax.Precision.HIGHEST
PAD = 8


def nt_dot(a, b, precision=None):
    return lax.dot_general(
        a, b, (((1,), (1,)), ((), ())), precision=precision, preferred_element_type=F32
    )


def iota(shape, axis):
    return lax.broadcasted_iota(jnp.int32, shape, axis)


def slab_step(temp, k0, ux, uy, uz, wall, t_nb, k_nb, u_nb):
    rows = temp.shape[0]
    row = iota(temp.shape, 0)
    out = temp
    for pos, (sign, own) in enumerate(((1, ux), (-1, ux), (1, uy), (-1, uy))):
        kk, uu, n = k0 + k_nb[pos], own + u_nb[pos], t_nb[pos]
        out = out + kk * (n - temp) - sign * uu * (temp + n)
    up = pltpu.roll(temp, rows - 1, 0)
    kk, uu = k0 + pltpu.roll(k0, rows - 1, 0), uz + pltpu.roll(uz, rows - 1, 0)
    out = out + kk * (up - temp) - uu * (temp + up)
    first = row == 0
    down = jnp.where(first, wall, pltpu.roll(temp, 1, 0))
    kk = k0 + jnp.where(first, 0.0, pltpu.roll(k0, 1, 0))
    uu = uz + jnp.where(first, 0.0, pltpu.roll(uz, 1, 0))
    return out + kk * (down - temp) + uu * (temp + down)


def kernel(
    ngx, ngy,
    t_hbm, k_hbm, v_hbm, wall_ref, count_ref, map_ref, st_ref, sc_ref, cool_ref,
    fluid_ref, wallout_ref, solid_ref,
    tp, t1p, kp, uxp, uyp, uzp, coef, kraw, vraw, wallb,
    ys_send, ys_recv, y1_send, y1_recv,
    wy_send, wy_recv, wx_send, wx_recv, vy_send, vy_recv, vx_send, vx_recv,
    cbuf, csend, cc, nb, m3s, m3r, surf,
    ld_sem, hs, hr, t1s, t1r, ws, wr, v2s, v2r, gs, gr, out_sem, rel,
):
    nx, ny, nz = t_hbm.shape
    cells = nx * ny
    nblk = cells // 128
    ndev = ngx * ngy
    nsolid = 2 * ndev
    i, j = lax.axis_index("gx"), lax.axis_index("gy")
    me = i * ngy + j

    def gxd(k):
        return (lax.rem(i + k + ngx, ngx), j)

    def gyd(k):
        return (i, lax.rem(j + k + ngy, ngy))

    def hello(sem, targets):
        for target in targets:
            pl.semaphore_signal(sem, inc=1, device_id=target, device_id_type=MESH)

    barrier = pltpu.get_barrier_semaphore()
    near4 = [gxd(1), gxd(-1), gyd(1), gyd(-1)]
    hello(barrier, near4)
    inside = (pl.ds(1, nx), pl.ds(PAD, ny), slice(None))
    load_k = pltpu.make_async_copy(k_hbm, kraw, ld_sem.at[0])
    load_v = pltpu.make_async_copy(v_hbm, vraw, ld_sem.at[1])
    load_t = pltpu.make_async_copy(t_hbm, tp.at[inside], ld_sem.at[2])
    load_t.start()
    load_k.start()
    load_v.start()

    eye = iota((ny, ny), 0) == iota((ny, ny), 1)

    def wall_body(x, carry):
        line = wall_ref[pl.ds(x, 1), :]
        col = jnp.sum(jnp.where(eye, jnp.broadcast_to(line, (ny, ny)), 0.0), axis=1, keepdims=True)
        wallb[x] = jnp.broadcast_to(col, (ny, 128))
        return carry

    lax.fori_loop(0, nx, wall_body, 0)

    for cond, plane in ((i == 0, 0), (i == ngx - 1, nx + 1)):

        @pl.when(cond)
        def _():
            tp[plane] = jnp.zeros(tp.shape[1:], F32)
            t1p[plane] = jnp.zeros(t1p.shape[1:], F32)
            kp[plane] = jnp.zeros(kp.shape[1:], F32)
            uxp[plane] = jnp.zeros(uxp.shape[1:], F32)
            side = 0 if plane == 0 else 1
            wx_recv[side] = jnp.zeros(wx_recv.shape[1:], F32)
            vx_recv[side] = jnp.zeros(vx_recv.shape[1:], F32)

    for cond, side in ((j == 0, 0), (j == ngy - 1, 1)):

        @pl.when(cond)
        def _():
            ys_recv[side] = jnp.zeros(ys_recv.shape[1:], F32)
            y1_recv[side] = jnp.zeros(y1_recv.shape[1:], F32)
            wy_recv[side] = jnp.zeros(wy_recv.shape[1:], F32)
            vy_recv[side] = jnp.zeros(vy_recv.shape[1:], F32)

    pl.semaphore_wait(barrier, 4)
    hello(rel.at[0], near4)

    def halo(src_of, dst_of, send, recv, axis):
        def make(up):
            spot, size, dev = (i, ngx, gxd) if axis == 0 else (j, ngy, gyd)
            copy = pltpu.make_async_remote_copy(
                src_ref=src_of(up), dst_ref=dst_of(up),
                send_sem=send.at[up], recv_sem=recv.at[up],
                device_id=dev(1 if up else -1), device_id_type=MESH,
            )
            sends = spot < size - 1 if up else spot > 0
            gets = spot > 0 if up else spot < size - 1
            return copy, sends, gets

        pairs = [make(1), make(0)]

        def start():
            for copy, sends, gets in pairs:
                pl.when(sends)(copy.start)

        def wait_recv():
            for copy, sends, gets in pairs:
                pl.when(gets)(copy.wait_recv)

        def wait_send():
            for copy, sends, gets in pairs:
                pl.when(sends)(copy.wait_send)

        return start, wait_recv, wait_send

    wy = halo(lambda up: wy_send, lambda up: wy_recv.at[1 - up], ws.at[0], wr.at[0], 1)
    wx = halo(lambda up: wx_send.at[up], lambda up: wx_recv.at[1 - up], ws.at[1], wr.at[1], 0)
    vy = halo(lambda up: vy_send, lambda up: vy_recv.at[1 - up], v2s.at[0], v2r.at[0], 1)
    vx = halo(lambda up: vx_send.at[up], lambda up: vx_recv.at[1 - up], v2s.at[1], v2r.at[1], 0)
    ys = halo(lambda up: ys_send.at[up], lambda up: ys_recv.at[1 - up], hs.at[0], hr.at[0], 1)

    def planes(ref, padded):
        rows = pl.ds(PAD, ny) if padded else pl.ds(0, ny)
        return (
            lambda up: ref.at[nx if up else 1, rows],
            lambda up: ref.at[0 if up else nx + 1, rows],
        )

    xt = halo(*planes(tp, True), hs.at[1], hr.at[1], 0)
    xk = halo(*planes(kp, True), hs.at[2], hr.at[2], 0)
    xu = halo(*planes(uxp, False), hs.at[3], hr.at[3], 0)
    y1 = halo(lambda up: y1_send.at[up], lambda up: y1_recv.at[1 - up], t1s.at[0], t1r.at[0], 1)
    x1 = halo(*planes(t1p, True), t1s.at[1], t1r.at[1], 0)

    load_t.wait()
    load_k.wait()
    load_v.wait()
    xt[0]()

    pick = (iota((8, 128), 0) == iota((8, 128), 1)).astype(F32)
    pick16 = pick.astype(jnp.bfloat16)

    def slab(value, exact):
        value = value.reshape(cells, 128)
        return nt_dot(pick, value, EXACT) if exact else nt_dot(pick16, value)

    s_t = slab(tp[1 : nx + 1, PAD : PAD + ny, 0:128], True)
    s_w = slab(wallb[...], True)[0:1]
    s_k = 0.5 * slab(kraw[:, :, 0:128], False)
    s_ux = 0.25 * slab(vraw[0, :, :, 0:128], False)
    s_uy = 0.25 * slab(vraw[1, :, :, 0:128], False)
    s_uz = 0.25 * slab(vraw[2, :, :, 0:128], False)
    wy_send[0:2, :] = s_t[0:2]
    wy_send[2:4, :] = s_k[0:2]
    wy_send[4:6, :] = s_uy[0:2]
    wy_send[6:8, :] = jnp.zeros((2, cells), F32)
    for up, lanes in ((1, slice(cells - 128, cells)), (0, slice(0, 128))):
        wx_send[up, 0:2, :] = s_t[0:2, lanes]
        wx_send[up, 2:4, :] = s_k[0:2, lanes]
        wx_send[up, 4:6, :] = s_ux[0:2, lanes]
        wx_send[up, 6:8, :] = jnp.zeros((2, 128), F32)
    wy[0]()
    wx[0]()

    pl.semaphore_wait(rel.at[0], 4)
    hello(rel.at[1], [gxd(2), gxd(-2), gyd(2), gyd(-2)])

    def convert(x, carry):
        kv = 0.5 * kraw[x].astype(F32)
        kp[x + 1, PAD : PAD + ny, :] = kv
        uxp[x + 1] = 0.25 * vraw[0, x].astype(F32)
        uv = 0.25 * vraw[1, x].astype(F32)
        uyp[x, PAD : PAD + ny, :] = uv
        uzp[x] = 0.25 * vraw[2, x].astype(F32)
        ys_send[0, 0, x] = tp[x + 1, PAD : PAD + 1, :]
        ys_send[1, 0, x] = tp[x + 1, PAD + ny - 1 : PAD + ny, :]
        ys_send[0, 1, x] = kv[0:1]
        ys_send[1, 1, x] = kv[ny - 1 : ny]
        ys_send[0, 2, x] = uv[0:1]
        ys_send[1, 2, x] = uv[ny - 1 : ny]
        return carry

    lax.fori_loop(0, nx, convert, 0)
    ys[0]()
    xk[0]()
    xu[0]()

    pl.semaphore_wait(rel.at[1], 4)
    hello(rel.at[2], [gyd(4), gyd(-4)])

    counts = jnp.full((8, 128), count_ref[0], jnp.int32).astype(F32)
    csend[...] = counts

    def spread(src, buf, slot, size, dev, sem, rsem):
        for k in range(1, size):
            pltpu.make_async_remote_copy(
                src_ref=src(k), dst_ref=buf.at[slot], send_sem=sem, recv_sem=rsem,
                device_id=dev(k), device_id_type=MESH,
            ).start()

    def all_in(buf, size, sem):
        part = buf.at[pl.ds(0, size - 1)]
        pltpu.make_async_copy(part, part, sem).wait()

    spread(lambda k: csend, cbuf, i, ngx, gxd, gs.at[0], gr.at[0])

    lane = iota((8, cells), 1)
    y_first, y_last = lax.rem(lane, ny) == 0, lax.rem(lane, ny) == ny - 1
    x_first, x_last = lane < ny, lane >= cells - ny

    def y_neighbours(own, low, high):
        plus = jnp.where(y_last, pltpu.roll(high, ny - 1, 1), pltpu.roll(own, cells - 1, 1))
        minus = jnp.where(y_first, pltpu.roll(low, cells - (ny - 1), 1), pltpu.roll(own, 1, 1))
        return plus, minus

    def widen(tile):
        return jnp.concatenate([tile] * (cells // 128), axis=1)

    def x_neighbours(own, low, high):
        plus = jnp.where(x_last, widen(pltpu.roll(high, 128 - ny, 1)), pltpu.roll(own, cells - ny, 1))
        minus = jnp.where(x_first, widen(pltpu.roll(low, ny, 1)), pltpu.roll(own, ny, 1))
        return plus, minus

    wy[1]()
    wx[1]()

    def rows_of(value, part):
        return pltpu.roll(value, 8 - 2 * part, 0) if part else value

    ylow, yhigh, xlow, xhigh = wy_recv[0], wy_recv[1], wx_recv[0], wx_recv[1]
    ty = y_neighbours(s_t, rows_of(ylow, 0), rows_of(yhigh, 0))
    ky = y_neighbours(s_k, rows_of(ylow, 1), rows_of(yhigh, 1))
    uy = y_neighbours(s_uy, rows_of(ylow, 2), rows_of(yhigh, 2))
    tx = x_neighbours(s_t, rows_of(xlow, 0), rows_of(xhigh, 0))
    kx = x_neighbours(s_k, rows_of(xlow, 1), rows_of(xhigh, 1))
    ux = x_neighbours(s_ux, rows_of(xlow, 2), rows_of(xhigh, 2))
    k_nb, u_nb = kx + ky, ux + uy
    first = slab_step(s_t, s_k, s_ux, s_uy, s_uz, s_w, tx + ty, k_nb, u_nb)
    vy_send[...] = first
    vx_send[1] = first[:, cells - 128 :]
    vx_send[0] = first[:, 0:128]
    vy[0]()
    vx[0]()

    cbuf[i] = counts
    cond_blocks = jnp.concatenate([s_k[0:1, 128 * b : 128 * b + 128] for b in range(nblk)], axis=0)
    all_in(cbuf, ngx, gr.at[0])
    row8 = iota((8, 128), 0)
    column = jnp.zeros((8, 128), F32)
    for k in range(ngx):
        column = column + jnp.where(row8 == k, cbuf[k], 0.0)
    cc[j, 0:8] = cond_blocks
    cc[j, 8:16] = column
    pl.semaphore_wait(rel.at[2], 2)
    spread(lambda k: cc.at[j], cc, j, ngy, gyd, gs.at[1], gr.at[1])

    vy[1]()
    vx[1]()
    ty = y_neighbours(first, vy_recv[0], vy_recv[1])
    tx = x_neighbours(first, vx_recv[0], vx_recv[1])
    second = slab_step(first, s_k, s_ux, s_uy, s_uz, s_w, tx + ty, k_nb, u_nb)
    nb[j] = jnp.concatenate([second[0:1, 128 * b : 128 * b + 128] for b in range(nblk)], axis=0)
    spread(lambda k: nb.at[j], nb, j, ngy, gyd, gs.at[2], gr.at[2])

    ys[1]()
    xk[1]()
    xu[1]()
    zlane = iota((8, nz), 1)
    z_first, z_last = zlane == 0, zlane == nz - 1

    def coef_body(x, carry):
        kp[x + 1, PAD - 1 : PAD, :] = ys_recv[0, 1, x]
        kp[x + 1, PAD + ny : PAD + ny + 1, :] = ys_recv[1, 1, x]
        uyp[x, PAD - 1 : PAD, :] = ys_recv[0, 2, x]
        uyp[x, PAD + ny : PAD + ny + 1, :] = ys_recv[1, 2, x]
        tp[x + 1, PAD - 1 : PAD, :] = ys_recv[0, 0, x]
        tp[x + 1, PAD + ny : PAD + ny + 1, :] = ys_recv[1, 0, x]
        for yt in range(0, ny, 8):
            y0 = PAD + yt
            k0 = kp[x + 1, y0 : y0 + 8, :]
            ux0 = uxp[x + 1, yt : yt + 8, :]
            uy0 = uyp[x, y0 : y0 + 8, :]
            uz0 = uzp[x, yt : yt + 8, :]
            here = pl.ds(yt, 8)
            kk, uu = k0 + kp[x + 2, y0 : y0 + 8, :], ux0 + uxp[x + 2, yt : yt + 8, :]
            coef[1, x, here] = kk - uu
            total = kk + uu
            kk, uu = k0 + kp[x, y0 : y0 + 8, :], ux0 + uxp[x, yt : yt + 8, :]
            coef[2, x, here] = kk + uu
            total = total + (kk - uu)
            kk, uu = k0 + kp[x + 1, y0 + 1 : y0 + 9, :], uy0 + uyp[x, y0 + 1 : y0 + 9, :]
            coef[3, x, here] = kk - uu
            total = total + (kk + uu)
            kk, uu = k0 + kp[x + 1, y0 - 1 : y0 + 7, :], uy0 + uyp[x, y0 - 1 : y0 + 7, :]
            coef[4, x, here] = kk + uu
            total = total + (kk - uu)
            kk = k0 + jnp.where(z_last, 0.0, pltpu.roll(k0, nz - 1, 1))
            uu = uz0 + jnp.where(z_last, 0.0, pltpu.roll(uz0, nz - 1, 1))
            coef[5, x, here] = jnp.where(z_last, 0.0, kk - uu)
            total = total + (kk + uu)
            kk = k0 + jnp.where(z_first, 0.0, pltpu.roll(k0, 1, 1))
            uu = uz0 + jnp.where(z_first, 0.0, pltpu.roll(uz0, 1, 1))
            coef[6, x, here] = kk + uu
            total = total + (kk - uu)
            coef[0, x, here] = 1.0 - total
        return carry

    lax.fori_loop(0, nx, coef_body, 0)

    def step_at(src, x, yt):
        y0 = PAD + yt
        here = pl.ds(yt, 8)
        mid = src[x + 1, y0 : y0 + 8, :]
        wall = jnp.concatenate([wallb[x, here]] * (nz // 128), axis=1)
        down = jnp.where(z_first, wall, pltpu.roll(mid, 1, 1))
        out = coef[0, x, here] * mid
        out = out + coef[1, x, here] * src[x + 2, y0 : y0 + 8, :]
        out = out + coef[2, x, here] * src[x, y0 : y0 + 8, :]
        out = out + coef[3, x, here] * src[x + 1, y0 + 1 : y0 + 9, :]
        out = out + coef[4, x, here] * src[x + 1, y0 - 1 : y0 + 7, :]
        out = out + coef[5, x, here] * pltpu.roll(mid, nz - 1, 1)
        return out + coef[6, x, here] * down

    xt[1]()

    def first_body(x, carry):
        for yt in range(0, ny, 8):
            value = step_at(tp, x, yt)
            t1p[x + 1, PAD + yt : PAD + yt + 8, :] = value
            if yt == 0:
                y1_send[0, x] = value[0:1]
            if yt == ny - 8:
                y1_send[1, x] = value[7:8]
        return carry

    lax.fori_loop(0, nx, first_body, 0)
    y1[0]()
    x1[0]()

    all_in(cc, ngy, gr.at[1])
    q = iota((8, 128), 1)
    table = jnp.zeros((8, 128), F32)
    for k in range(ngy):
        table = table + jnp.where(q // nblk == k, cc[k, 8:16], 0.0)
    before = (iota((128, 128), 0) // nblk < iota((128, 128), 1) // nblk).astype(F32) * (1.0 / nblk)
    prefix = jnp.dot(table, before, precision=EXACT, preferred_element_type=F32)
    row_total = jnp.sum(table, axis=1, keepdims=True) * (1.0 / nblk)
    offset = jnp.sum(
        jnp.where(row8 == i, prefix, 0.0) + jnp.where(row8 < i, jnp.broadcast_to(row_total, (8, 128)), 0.0),
        axis=0, keepdims=True,
    )
    mine = jnp.sum(jnp.where(row8 == i, table, 0.0), axis=0, keepdims=True)
    slot = lax.rem(iota((1, 128), 1), nblk).astype(F32)
    live = slot < mine
    rank = jnp.where(live, offset + slot, -1.0)
    onehot = (iota((nsolid, 128), 0).astype(F32) == rank).astype(F32)
    fmap = map_ref[...].astype(F32)
    target = jnp.dot(fmap, onehot, precision=EXACT, preferred_element_type=F32)
    target = jnp.where(live, target, -1.0)
    line = iota((8 * ngx, 128), 0)
    kind = lax.rem(line, 8)
    owner = 2 * ((line // 8) * ngy + j)
    for_near = jnp.where(kind < 2, owner + kind, -2).astype(F32)
    for_cond = jnp.where((kind >= 2) & (kind < 4), owner + kind - 2, -2).astype(F32)
    w_near = (for_near == target).astype(F32)
    w_cond = (for_cond == target).astype(F32)
    cond_rows = cc[:, 0:8].reshape(ngy * 8, 128)
    payload_c = jnp.dot(w_cond[:, : ngy * 8], cond_rows, precision=EXACT, preferred_element_type=F32)

    all_in(nb, ngy, gr.at[2])
    payload = payload_c + jnp.dot(
        w_near[:, : ngy * 8], nb[...].reshape(ngy * 8, 128), precision=EXACT, preferred_element_type=F32
    )
    m3s[...] = payload.reshape(ngx, 8, 128)
    spread(lambda k: m3s.at[gxd(k)[0]], m3r, i, ngx, gxd, gs.at[3], gr.at[3])
    m3r[i] = m3s[i]

    y1[1]()
    x1[1]()

    def second_body(x, carry):
        t1p[x + 1, PAD - 1 : PAD, :] = y1_recv[0, x]
        t1p[x + 1, PAD + ny : PAD + ny + 1, :] = y1_recv[1, x]
        for yt in range(0, ny, 8):
            fluid_ref[x, pl.ds(yt, 8)] = step_at(t1p, x, yt)
        return carry

    lax.fori_loop(0, nx, second_body, 0)

    own = iota((8, 128), 1) // nblk == j
    start = jnp.sum(jnp.where((row8 == 0) & own, jnp.broadcast_to(offset, (8, 128)), 0.0)) * (1.0 / nblk)
    slot8 = iota((8, nsolid), 0)
    rank8 = jnp.where(slot8 < count_ref[0], start + slot8.astype(F32), -1.0)
    onehot8 = (iota((8, nsolid), 1).astype(F32) == rank8).astype(F32)
    gline = iota((nsolid, nsolid), 0)
    gid = (2 * lax.rem(gline, ndev) + gline // ndev).astype(F32)
    holds = (gid == fmap).astype(F32)
    fetch = nt_dot(onehot8, holds)

    layers, width = st_ref.shape[1:]
    lines = 2 * layers
    conds = sc_ref[...].reshape(lines, width)
    temps = st_ref[...].reshape(lines, width)
    srow = lax.rem(iota((lines, width), 0), layers)
    scol = iota((lines, width), 1)
    c_up = jnp.where(srow == 0, 0.0, 0.5 * (conds + pltpu.roll(conds, 1, 0)))
    c_dn = jnp.where(srow == layers - 1, 0.0, 0.5 * (conds + pltpu.roll(conds, lines - 1, 0)))
    c_lf = jnp.where(scol == 0, 0.0, 0.5 * (conds + pltpu.roll(conds, 1, 1)))
    c_rt = jnp.where(scol == width - 1, 0.0, 0.5 * (conds + pltpu.roll(conds, width - 1, 1)))
    cool = cool_ref[...]

    def per_block(a, b):
        return jnp.concatenate(
            [jnp.broadcast_to(a, (layers, width)), jnp.broadcast_to(b, (layers, width))], axis=0
        )

    cool_at = per_block(cool[0:1], cool[1:2])

    all_in(m3r, ngx, gr.at[3])
    arrived = m3r[0]
    for k in range(1, ngx):
        arrived = arrived + m3r[k]
    heat = WALL_RATIO * arrived[2:4]
    flux = heat * arrived[0:2]
    is_wall, is_cool = srow == 0, srow == layers - 1
    bound = jnp.where(is_wall, per_block(heat[0:1], heat[1:2]), jnp.where(is_cool, COOL, 0.0))
    source = jnp.where(is_wall, per_block(flux[0:1], flux[1:2]), jnp.where(is_cool, COOL * cool_at, 0.0))
    inverse = 1.0 / (c_up + c_dn + c_lf + c_rt + bound)
    for _ in range(SWEEPS):
        total = c_up * pltpu.roll(temps, 1, 0) + c_dn * pltpu.roll(temps, lines - 1, 0)
        total = total + c_lf * pltpu.roll(temps, 1, 1) + c_rt * pltpu.roll(temps, width - 1, 1)
        temps = (total + source) * inverse
    surf[me] = jnp.concatenate([temps[0:1], temps[layers : layers + 1]], axis=0)

    def send_surface(k, carry):
        dev = lax.rem(me + k, ndev)
        pltpu.make_async_remote_copy(
            src_ref=surf.at[me], dst_ref=surf.at[me], send_sem=gs.at[4], recv_sem=gr.at[4],
            device_id=(dev // ngy, lax.rem(dev, ngy)), device_id_type=MESH,
        ).start()
        return carry

    lax.fori_loop(1, ndev, send_surface, 0)
    solid_ref[...] = temps.reshape(2, layers, width)

    for group in (wy, wx, vy, vx, ys, xt, xk, xu, y1, x1):
        group[2]()
    all_in(cbuf, ngx, gs.at[0])
    all_in(cc, ngy, gs.at[1])
    all_in(nb, ngy, gs.at[2])
    all_in(m3r, ngx, gs.at[3])
    all_in(surf, ndev, gs.at[4])

    all_in(surf, ndev, gr.at[4])
    back = jnp.dot(fetch[:, :ndev], surf[:, 0, :], precision=EXACT, preferred_element_type=F32)
    back = back + jnp.dot(fetch[:, ndev:], surf[:, 1, :], precision=EXACT, preferred_element_type=F32)
    per = 128 // ny
    lines_out = []
    shifted = [back if s == 0 else pltpu.roll(back, 128 - s * ny, 1) for s in range(per)]
    for x in range(nx):
        lines_out.append(shifted[x % per][x // per : x // per + 1, 0:ny])
    full = jnp.concatenate(lines_out, axis=0)
    is_live = iota((nx, ny), 0) // per < count_ref[0]
    wallout_ref[...] = jnp.where(is_live, full, wall_ref[...])


def solution(mesh):
    ngx, ngy = mesh.shape["gx"], mesh.shape["gy"]

    def shards(temp, kappa, vel, wall, count, fmap, stemp, scond, cool):
        nx, ny, nz = temp.shape
        cells, ndev = nx * ny, ngx * ngy
        vmem = pl.BlockSpec(memory_space=pltpu.VMEM)
        hbm = pl.BlockSpec(memory_space=pl.ANY)
        padded = (nx + 2, ny + 2 * PAD, nz)
        dma = pltpu.SemaphoreType.DMA
        out = pl.pallas_call(
            functools.partial(kernel, ngx, ngy),
            out_shape=(
                jax.ShapeDtypeStruct(temp.shape, F32),
                jax.ShapeDtypeStruct(wall.shape, F32),
                jax.ShapeDtypeStruct(stemp.shape, F32),
            ),
            in_specs=[hbm, hbm, hbm, vmem, pl.BlockSpec(memory_space=pltpu.SMEM), vmem, vmem, vmem, vmem],
            out_specs=(vmem, vmem, vmem),
            scratch_shapes=[
                pltpu.VMEM(padded, F32),
                pltpu.VMEM(padded, F32),
                pltpu.VMEM(padded, F32),
                pltpu.VMEM((nx + 2, ny, nz), F32),
                pltpu.VMEM((nx, ny + 2 * PAD, nz), F32),
                pltpu.VMEM((nx, ny, nz), F32),
                pltpu.VMEM((7, nx, ny, nz), F32),
                pltpu.VMEM((nx, ny, nz), jnp.bfloat16),
                pltpu.VMEM((3, nx, ny, nz), jnp.bfloat16),
                pltpu.VMEM((nx, ny, 128), F32),
                pltpu.VMEM((2, 3, nx, 1, nz), F32),
                pltpu.VMEM((2, 3, nx, 1, nz), F32),
                pltpu.VMEM((2, nx, 1, nz), F32),
                pltpu.VMEM((2, nx, 1, nz), F32),
                pltpu.VMEM((8, cells), F32),
                pltpu.VMEM((2, 8, cells), F32),
                pltpu.VMEM((2, 8, 128), F32),
                pltpu.VMEM((2, 8, 128), F32),
                pltpu.VMEM((8, cells), F32),
                pltpu.VMEM((2, 8, cells), F32),
                pltpu.VMEM((2, 8, 128), F32),
                pltpu.VMEM((2, 8, 128), F32),
                pltpu.VMEM((ngx, 8, 128), F32),
                pltpu.VMEM((8, 128), F32),
                pltpu.VMEM((ngy, 16, 128), F32),
                pltpu.VMEM((ngy, 8, 128), F32),
                pltpu.VMEM((ngx, 8, 128), F32),
                pltpu.VMEM((ngx, 8, 128), F32),
                pltpu.VMEM((ndev, 2, 128), F32),
                dma((3,)),
                dma((4, 2)),
                dma((4, 2)),
                dma((2, 2)),
                dma((2, 2)),
                dma((2, 2)),
                dma((2, 2)),
                dma((2, 2)),
                dma((2, 2)),
                dma((5,)),
                dma((5,)),
                dma((1,)),
                pltpu.SemaphoreType.REGULAR((3,)),
            ],
            compiler_params=pltpu.CompilerParams(
                collective_id=0, has_side_effects=True, vmem_limit_bytes=60 << 20
            ),
            name="coupled_step",
        )(temp, kappa, vel, wall, count, fmap.reshape(1, -1), stemp, scond, cool)
        return out

    return jax.shard_map(
        shards,
        mesh=mesh,
        in_specs=(
            P("gx", "gy", None),
            P("gx", "gy", None),
            P(None, "gx", "gy", None),
            P("gx", "gy"),
            P(("gx", "gy")),
            P(),
            P(("gx", "gy"), None, None),
            P(("gx", "gy"), None, None),
            P(("gx", "gy"), None),
        ),
        out_specs=(P("gx", "gy", None), P("gx", "gy"), P(("gx", "gy"), None, None)),
        check_vma=False,
    )
```

time: 453 us -> 51.5 us (0.11)
  blocking collectives: 187 us -> 0 us
  local copies, waits for them, and re-layouts: 103 us -> 4.42 us
  loops' own time: 74.6 us -> 0 us
  Pallas kernels: 0 us -> 45.6 us
  starting transfers between devices: 34.1 us -> 0 us
  other arithmetic: 33 us -> 0 us
  between operations: 15.4 us -> 1.3 us
    unnamed x2 -> x0, blocking collectives: 138 us -> none
    another operation x1 -> x0, loops' own time: 74.6 us -> none  [entering(): return lax.fori_loop(0, count, turn, start)]
    dynamic_slice x128 -> x0, local copies, waits for them, and re-layouts: 73.9 us -> none  [turn(): new = combine(before, everything[k])]
    all_gather x1 -> x0, blocking collectives: 49.7 us -> none  [shards(): piece = lax.all_gather(surface, ('gx', 'gy'), axis=0, tiled=True)]
    pallas_call x0 -> x1, Pallas kernels: none -> 45.6 us  [shards(): pl.pallas_call(functools.partial(kernel, ngx, ngy), out_shape=(jax.ShapeD...]
    ppermute x12 -> x0, starting transfers between devices: 34 us -> none  [the longest x6 24.2 us: with_halo(): lax.ppermute(lax.slice_in_dim(block, block.shape[dim] - width, None, axis...]
    add x2 -> x0, other arithmetic: 23.1 us -> none  [advance(): updated + face_term(center, cond_mid, lower, cond_down, flow_down, mid_z,...]
    slice x25 -> x0, local copies, waits for them, and re-layouts: 11 us -> none  [the longest x1 4.76 us: advance(): flow_down = jnp.concatenate([zero_col, mid_z[..., :-1]], axis=-1)]
  transfers between devices with their start and end apart: 13 -> 0, of which waited for: 2 -> 0; matrix products, arithmetic and copies ran while one was open for 22% -> 0% of each run, Pallas kernels for 0% -> 0%
where the time goes in v1:
time: 51.5 us; the launch traced here: 51.3 us
  Pallas kernels  45.6 us (89%)
  local copies, waits for them, and re-layouts  4.42 us (9%)
  between operations  1.3 us (3%)
    pallas_call x1, Pallas kernels, shards(): pl.pallas_call(functools.partial(kernel, ngx, ngy), out_shape=(jax.ShapeD...  45.6 us
    unnamed x7, local copies, waits for them, and re-layouts  4.42 us

profile of v1, /device:TPU:1, one launch (start us, length us, event | category | flops | bytes accessed | tf_op | source)
XLA Modules:
  0.0 51.3 jit_solution(8272306871813502151)
XLA Ops:
  1.3 45.6 %coupled_step.1 = (f32[32,32,512]{2,1,0:T(8,128)}, f32[32,32]{1,0:T(8,128)}, f32[2,32,128]{2,1,0:T(8,128)}) custom-call(f32[32,32,512]{2,1,0:T(8,128)} %t_hbm.1, bf16[32,32,512]{2,1,0:T(8,128)(2,1)} %k_hbm.1, bf16[3,32,32,512]{3,2,1,0:T(8,128)(2,1)} %v_hbm.1, f32[32,32]{1,0:T(8,128)} %wall_ref.1, s32[1]{0:T(128)S(6)} %copy.15.count_ref, s32[1,256]{1,0:T(1,128)} %bitcast.1, ...), custom_call_target="tpu_custom_call" | custom-call | tf_op jit(solution)/shard_map/coupled_step/pallas_call | solution.py:508
  46.8 0.0 copy-start.1
  46.9 0.0 copy-start
  46.9 3.2 %copy.16 = f32[32,32,512]{2,1,0:T(8,128)} copy(f32[32,32,512]{2,1,0:T(8,128)} %get-tuple-element.6) | data formatting | bytes 4194304
  50.1 0.0 copy-done.1
  50.1 0.6 %copy.17 = f32[32,32]{1,0:T(8,128)} copy(f32[32,32]{1,0:T(8,128)S(1)} %copy-done.1) | data formatting | bytes 8192
  50.7 0.0 copy-done
  50.7 0.6 %copy.18 = f32[2,32,128]{2,1,0:T(8,128)} copy(f32[2,32,128]{2,1,0:T(8,128)S(1)} %copy-done) | data formatting | bytes 65536
Async XLA Ops:
  46.8 3.2 %copy-start.1 = (f32[32,32]{1,0:T(8,128)S(1)}, f32[32,32]{1,0:T(8,128)}, u32[]{:S(2)}) copy-start(f32[32,32]{1,0:T(8,128)} %get-tuple-element.7) | copy-start | bytes 12292
  46.9 3.8 %copy-start = (f32[2,32,128]{2,1,0:T(8,128)S(1)}, f32[2,32,128]{2,1,0:T(8,128)}, u32[]{:S(2)}) copy-start(f32[2,32,128]{2,1,0:T(8,128)} %get-tuple-element.8) | copy-start | bytes 98308

commit v2 on v1

--- a/solution.py
+++ b/solution.py
@@ -43,6 +43,23 @@
     return out + kk * (down - temp) + uu * (temp + down)
 
 
+def conductances(conds, layers):
+    lines, width = conds.shape
+    row, col = lax.rem(iota(conds.shape, 0), layers), iota(conds.shape, 1)
+    up = jnp.where(row == 0, 0.0, 0.5 * (conds + pltpu.roll(conds, 1, 0)))
+    down = jnp.where(row == layers - 1, 0.0, 0.5 * (conds + pltpu.roll(conds, lines - 1, 0)))
+    left = jnp.where(col == 0, 0.0, 0.5 * (conds + pltpu.roll(conds, 1, 1)))
+    right = jnp.where(col == width - 1, 0.0, 0.5 * (conds + pltpu.roll(conds, width - 1, 1)))
+    return up, down, left, right
+
+
+def sweep(temps, up, down, left, right, source, inverse):
+    lines, width = temps.shape
+    total = up * pltpu.roll(temps, 1, 0) + down * pltpu.roll(temps, lines - 1, 0)
+    total = total + left * pltpu.roll(temps, 1, 1) + right * pltpu.roll(temps, width - 1, 1)
+    return (total + source) * inverse
+
+
 def kernel(
     ngx, ngy,
     t_hbm, k_hbm, v_hbm, wall_ref, count_ref, map_ref, st_ref, sc_ref, cool_ref,
@@ -50,8 +67,8 @@
     tp, t1p, kp, uxp, uyp, uzp, coef, kraw, vraw, wallb,
     ys_send, ys_recv, y1_send, y1_recv,
     wy_send, wy_recv, wx_send, wx_recv, vy_send, vy_recv, vx_send, vx_recv,
-    cbuf, csend, cc, nb, m3s, m3r, surf,
-    ld_sem, hs, hr, t1s, t1r, ws, wr, v2s, v2r, gs, gr, out_sem, rel,
+    cbuf, csend, cc, nb, m3s, m3r, tops, m5s, m5r,
+    ld_sem, hs, hr, t1s, t1r, ws, wr, v2s, v2r, gs, gr,
 ):
     nx, ny, nz = t_hbm.shape
     cells = nx * ny
@@ -67,20 +84,21 @@
     def gyd(k):
         return (i, lax.rem(j + k + ngy, ngy))
 
-    def hello(sem, targets):
-        for target in targets:
-            pl.semaphore_signal(sem, inc=1, device_id=target, device_id_type=MESH)
-
     barrier = pltpu.get_barrier_semaphore()
-    near4 = [gxd(1), gxd(-1), gyd(1), gyd(-1)]
-    hello(barrier, near4)
-    inside = (pl.ds(1, nx), pl.ds(PAD, ny), slice(None))
-    load_k = pltpu.make_async_copy(k_hbm, kraw, ld_sem.at[0])
-    load_v = pltpu.make_async_copy(v_hbm, vraw, ld_sem.at[1])
-    load_t = pltpu.make_async_copy(t_hbm, tp.at[inside], ld_sem.at[2])
-    load_t.start()
-    load_k.start()
-    load_v.start()
+    peers = [gxd(k) for k in range(1, ngx)] + [gyd(k) for k in range(1, ngy)]
+    for peer in peers:
+        pl.semaphore_signal(barrier, inc=1, device_id=peer, device_id_type=MESH)
+    loads = []
+    for part, zs in enumerate((pl.ds(0, 128), pl.ds(128, nz - 128))):
+        inside = (pl.ds(1, nx), pl.ds(PAD, ny), zs)
+        loads.append((
+            pltpu.make_async_copy(t_hbm.at[:, :, zs], tp.at[inside], ld_sem.at[0, part]),
+            pltpu.make_async_copy(k_hbm.at[:, :, zs], kraw.at[:, :, zs], ld_sem.at[1, part]),
+            pltpu.make_async_copy(v_hbm.at[:, :, :, zs], vraw.at[:, :, :, zs], ld_sem.at[2, part]),
+        ))
+    for group in loads:
+        for load in group:
+            load.start()
 
     eye = iota((ny, ny), 0) == iota((ny, ny), 1)
 
@@ -113,8 +131,7 @@
             wy_recv[side] = jnp.zeros(wy_recv.shape[1:], F32)
             vy_recv[side] = jnp.zeros(vy_recv.shape[1:], F32)
 
-    pl.semaphore_wait(barrier, 4)
-    hello(rel.at[0], near4)
+    s_w = jnp.concatenate([wall_ref[x : x + 1, :] for x in range(nx)], axis=1)
 
     def halo(src_of, dst_of, send, recv, axis):
         def make(up):
@@ -163,24 +180,41 @@
     y1 = halo(lambda up: y1_send.at[up], lambda up: y1_recv.at[1 - up], t1s.at[0], t1r.at[0], 1)
     x1 = halo(*planes(t1p, True), t1s.at[1], t1r.at[1], 0)
 
-    load_t.wait()
-    load_k.wait()
-    load_v.wait()
-    xt[0]()
-
-    pick = (iota((8, 128), 0) == iota((8, 128), 1)).astype(F32)
-    pick16 = pick.astype(jnp.bfloat16)
-
-    def slab(value, exact):
-        value = value.reshape(cells, 128)
-        return nt_dot(pick, value, EXACT) if exact else nt_dot(pick16, value)
-
-    s_t = slab(tp[1 : nx + 1, PAD : PAD + ny, 0:128], True)
-    s_w = slab(wallb[...], True)[0:1]
-    s_k = 0.5 * slab(kraw[:, :, 0:128], False)
-    s_ux = 0.25 * slab(vraw[0, :, :, 0:128], False)
-    s_uy = 0.25 * slab(vraw[1, :, :, 0:128], False)
-    s_uz = 0.25 * slab(vraw[2, :, :, 0:128], False)
+    for load in loads[0]:
+        load.wait()
+
+    counts = jnp.full((8, 128), count_ref[0], jnp.int32).astype(F32)
+    csend[...] = counts
+    tops[i, 0:16] = st_ref[:, 0:8].reshape(16, 128)
+    tops[i, 16:32] = sc_ref[:, 0:8].reshape(16, 128)
+
+    def spread(src, buf, slot, size, dev, sem, rsem):
+        for k in range(1, size):
+            pltpu.make_async_remote_copy(
+                src_ref=src(k), dst_ref=buf.at[slot], send_sem=sem, recv_sem=rsem,
+                device_id=dev(k), device_id_type=MESH,
+            ).start()
+
+    def all_in(buf, size, sem):
+        part = buf.at[pl.ds(0, size - 1)]
+        pltpu.make_async_copy(part, part, sem).wait()
+
+
+    pick16 = (iota((8, 128), 0) == iota((8, 128), 1)).astype(F32).astype(jnp.bfloat16)
+
+    def slab(value):
+        return nt_dot(pick16, value.reshape(cells, 128))
+
+    rest = tp[1 : nx + 1, PAD : PAD + ny, 0:128].reshape(cells, 128)
+    s_t = jnp.zeros((8, cells), F32)
+    for _ in range(3):
+        piece = rest.astype(jnp.bfloat16)
+        s_t = s_t + nt_dot(pick16, piece)
+        rest = rest - piece.astype(F32)
+    s_k = 0.5 * slab(kraw[:, :, 0:128])
+    s_ux = 0.25 * slab(vraw[0, :, :, 0:128])
+    s_uy = 0.25 * slab(vraw[1, :, :, 0:128])
+    s_uz = 0.25 * slab(vraw[2, :, :, 0:128])
     wy_send[0:2, :] = s_t[0:2]
     wy_send[2:4, :] = s_k[0:2]
     wy_send[4:6, :] = s_uy[0:2]
@@ -190,11 +224,13 @@
         wx_send[up, 2:4, :] = s_k[0:2, lanes]
         wx_send[up, 4:6, :] = s_ux[0:2, lanes]
         wx_send[up, 6:8, :] = jnp.zeros((2, 128), F32)
+    pl.semaphore_wait(barrier, len(peers))
     wy[0]()
     wx[0]()
-
-    pl.semaphore_wait(rel.at[0], 4)
-    hello(rel.at[1], [gxd(2), gxd(-2), gyd(2), gyd(-2)])
+    spread(lambda k: csend, cbuf, i, ngx, gxd, gs.at[0], gr.at[0])
+    spread(lambda k: tops.at[i], tops, i, ngx, gxd, gs.at[4], gr.at[4])
+    for load in loads[1]:
+        load.wait()
 
     def convert(x, carry):
         kv = 0.5 * kraw[x].astype(F32)
@@ -211,29 +247,11 @@
         ys_send[1, 2, x] = uv[ny - 1 : ny]
         return carry
 
-    lax.fori_loop(0, nx, convert, 0)
+    lax.fori_loop(0, nx, convert, 0, unroll=4)
     ys[0]()
     xk[0]()
     xu[0]()
-
-    pl.semaphore_wait(rel.at[1], 4)
-    hello(rel.at[2], [gyd(4), gyd(-4)])
-
-    counts = jnp.full((8, 128), count_ref[0], jnp.int32).astype(F32)
-    csend[...] = counts
-
-    def spread(src, buf, slot, size, dev, sem, rsem):
-        for k in range(1, size):
-            pltpu.make_async_remote_copy(
-                src_ref=src(k), dst_ref=buf.at[slot], send_sem=sem, recv_sem=rsem,
-                device_id=dev(k), device_id_type=MESH,
-            ).start()
-
-    def all_in(buf, size, sem):
-        part = buf.at[pl.ds(0, size - 1)]
-        pltpu.make_async_copy(part, part, sem).wait()
-
-    spread(lambda k: csend, cbuf, i, ngx, gxd, gs.at[0], gr.at[0])
+    xt[0]()
 
     lane = iota((8, cells), 1)
     y_first, y_last = lax.rem(lane, ny) == 0, lax.rem(lane, ny) == ny - 1
@@ -282,7 +300,6 @@
         column = column + jnp.where(row8 == k, cbuf[k], 0.0)
     cc[j, 0:8] = cond_blocks
     cc[j, 8:16] = column
-    pl.semaphore_wait(rel.at[2], 2)
     spread(lambda k: cc.at[j], cc, j, ngy, gyd, gs.at[1], gr.at[1])
 
     vy[1]()
@@ -336,7 +353,7 @@
             coef[0, x, here] = 1.0 - total
         return carry
 
-    lax.fori_loop(0, nx, coef_body, 0)
+    lax.fori_loop(0, nx, coef_body, 0, unroll=4)
 
     def step_at(src, x, yt):
         y0 = PAD + yt
@@ -364,7 +381,7 @@
                 y1_send[1, x] = value[7:8]
         return carry
 
-    lax.fori_loop(0, nx, first_body, 0)
+    lax.fori_loop(0, nx, first_body, 0, unroll=4)
     y1[0]()
     x1[0]()
 
@@ -395,49 +412,40 @@
     for_cond = jnp.where((kind >= 2) & (kind < 4), owner + kind - 2, -2).astype(F32)
     w_near = (for_near == target).astype(F32)
     w_cond = (for_cond == target).astype(F32)
-    cond_rows = cc[:, 0:8].reshape(ngy * 8, 128)
-    payload_c = jnp.dot(w_cond[:, : ngy * 8], cond_rows, precision=EXACT, preferred_element_type=F32)
+    cond_rows = cc[:, 0:8].reshape(128, 128)
+    payload_c = jnp.dot(w_cond, cond_rows, precision=EXACT, preferred_element_type=F32)
+
+    top_line = iota((128, 128), 0)
+    top_row = lax.rem(top_line, 8)
+    top_block = top_line // 8
+    top_id = jnp.where(top_row == 0, 2 * ((top_block // 2) * ngy + j) + lax.rem(top_block, 2), -2)
+    w_top = (top_id.astype(F32) == target).astype(F32)
+    w_back = jnp.transpose(w_top)
+    all_in(tops, ngx, gr.at[4])
+    top_t = tops[:, 0:16].reshape(128, 128)
+    top_c = tops[:, 16:32].reshape(128, 128)
+    top_up, top_dn, top_lf, top_rt = conductances(top_c, 8)
+    top_bound = WALL_RATIO * jnp.dot(w_top, cond_rows, precision=EXACT, preferred_element_type=F32)
+    top_inv = 1.0 / (top_up + top_dn + top_lf + top_rt + top_bound)
 
     all_in(nb, ngy, gr.at[2])
-    payload = payload_c + jnp.dot(
-        w_near[:, : ngy * 8], nb[...].reshape(ngy * 8, 128), precision=EXACT, preferred_element_type=F32
-    )
+    near_rows = nb[...].reshape(128, 128)
+    payload = payload_c + jnp.dot(w_near, near_rows, precision=EXACT, preferred_element_type=F32)
     m3s[...] = payload.reshape(ngx, 8, 128)
     spread(lambda k: m3s.at[gxd(k)[0]], m3r, i, ngx, gxd, gs.at[3], gr.at[3])
     m3r[i] = m3s[i]
-
-    y1[1]()
-    x1[1]()
-
-    def second_body(x, carry):
-        t1p[x + 1, PAD - 1 : PAD, :] = y1_recv[0, x]
-        t1p[x + 1, PAD + ny : PAD + ny + 1, :] = y1_recv[1, x]
-        for yt in range(0, ny, 8):
-            fluid_ref[x, pl.ds(yt, 8)] = step_at(t1p, x, yt)
-        return carry
-
-    lax.fori_loop(0, nx, second_body, 0)
-
-    own = iota((8, 128), 1) // nblk == j
-    start = jnp.sum(jnp.where((row8 == 0) & own, jnp.broadcast_to(offset, (8, 128)), 0.0)) * (1.0 / nblk)
-    slot8 = iota((8, nsolid), 0)
-    rank8 = jnp.where(slot8 < count_ref[0], start + slot8.astype(F32), -1.0)
-    onehot8 = (iota((8, nsolid), 1).astype(F32) == rank8).astype(F32)
-    gline = iota((nsolid, nsolid), 0)
-    gid = (2 * lax.rem(gline, ndev) + gline // ndev).astype(F32)
-    holds = (gid == fmap).astype(F32)
-    fetch = nt_dot(onehot8, holds)
+    top_src = top_bound * jnp.dot(w_top, near_rows, precision=EXACT, preferred_element_type=F32)
+    for _ in range(SWEEPS):
+        top_t = sweep(top_t, top_up, top_dn, top_lf, top_rt, top_src, top_inv)
+    m5s[...] = jnp.dot(w_back, top_t, precision=EXACT, preferred_element_type=F32).reshape(ngy, 8, 128)
+    spread(lambda k: m5s.at[gyd(k)[1]], m5r, j, ngy, gyd, gs.at[5], gr.at[5])
+    m5r[j] = m5s[j]
 
     layers, width = st_ref.shape[1:]
     lines = 2 * layers
-    conds = sc_ref[...].reshape(lines, width)
     temps = st_ref[...].reshape(lines, width)
     srow = lax.rem(iota((lines, width), 0), layers)
-    scol = iota((lines, width), 1)
-    c_up = jnp.where(srow == 0, 0.0, 0.5 * (conds + pltpu.roll(conds, 1, 0)))
-    c_dn = jnp.where(srow == layers - 1, 0.0, 0.5 * (conds + pltpu.roll(conds, lines - 1, 0)))
-    c_lf = jnp.where(scol == 0, 0.0, 0.5 * (conds + pltpu.roll(conds, 1, 1)))
-    c_rt = jnp.where(scol == width - 1, 0.0, 0.5 * (conds + pltpu.roll(conds, width - 1, 1)))
+    c_up, c_dn, c_lf, c_rt = conductances(sc_ref[...].reshape(lines, width), layers)
     cool = cool_ref[...]
 
     def per_block(a, b):
@@ -458,21 +466,20 @@
     source = jnp.where(is_wall, per_block(flux[0:1], flux[1:2]), jnp.where(is_cool, COOL * cool_at, 0.0))
     inverse = 1.0 / (c_up + c_dn + c_lf + c_rt + bound)
     for _ in range(SWEEPS):
-        total = c_up * pltpu.roll(temps, 1, 0) + c_dn * pltpu.roll(temps, lines - 1, 0)
-        total = total + c_lf * pltpu.roll(temps, 1, 1) + c_rt * pltpu.roll(temps, width - 1, 1)
-        temps = (total + source) * inverse
-    surf[me] = jnp.concatenate([temps[0:1], temps[layers : layers + 1]], axis=0)
-
-    def send_surface(k, carry):
-        dev = lax.rem(me + k, ndev)
-        pltpu.make_async_remote_copy(
-            src_ref=surf.at[me], dst_ref=surf.at[me], send_sem=gs.at[4], recv_sem=gr.at[4],
-            device_id=(dev // ngy, lax.rem(dev, ngy)), device_id_type=MESH,
-        ).start()
+        temps = sweep(temps, c_up, c_dn, c_lf, c_rt, source, inverse)
+    solid_ref[...] = temps.reshape(2, layers, width)
+
+    y1[1]()
+    x1[1]()
+
+    def second_body(x, carry):
+        t1p[x + 1, PAD - 1 : PAD, :] = y1_recv[0, x]
+        t1p[x + 1, PAD + ny : PAD + ny + 1, :] = y1_recv[1, x]
+        for yt in range(0, ny, 8):
+            fluid_ref[x, pl.ds(yt, 8)] = step_at(t1p, x, yt)
         return carry
 
-    lax.fori_loop(1, ndev, send_surface, 0)
-    solid_ref[...] = temps.reshape(2, layers, width)
+    lax.fori_loop(0, nx, second_body, 0, unroll=4)
 
     for group in (wy, wx, vy, vx, ys, xt, xk, xu, y1, x1):
         group[2]()
@@ -480,11 +487,13 @@
     all_in(cc, ngy, gs.at[1])
     all_in(nb, ngy, gs.at[2])
     all_in(m3r, ngx, gs.at[3])
-    all_in(surf, ndev, gs.at[4])
-
-    all_in(surf, ndev, gr.at[4])
-    back = jnp.dot(fetch[:, :ndev], surf[:, 0, :], precision=EXACT, preferred_element_type=F32)
-    back = back + jnp.dot(fetch[:, ndev:], surf[:, 1, :], precision=EXACT, preferred_element_type=F32)
+    all_in(tops, ngx, gs.at[4])
+    all_in(m5r, ngy, gs.at[5])
+
+    all_in(m5r, ngy, gr.at[5])
+    back = m5r[0]
+    for k in range(1, ngy):
+        back = back + m5r[k]
     per = 128 // ny
     lines_out = []
     shifted = [back if s == 0 else pltpu.roll(back, 128 - s * ny, 1) for s in range(per)]
@@ -493,6 +502,17 @@
     full = jnp.concatenate(lines_out, axis=0)
     is_live = iota((nx, ny), 0) // per < count_ref[0]
     wallout_ref[...] = jnp.where(is_live, full, wall_ref[...])
+
+
+def finish(fluid, wall, solid, fluid_ref, wall_ref, solid_ref, sem):
+    copies = [
+        pltpu.make_async_copy(src, dst, sem.at[n])
+        for n, (src, dst) in enumerate(((fluid, fluid_ref), (wall, wall_ref), (solid, solid_ref)))
+    ]
+    for copy in copies:
+        copy.start()
+    for copy in copies:
+        copy.wait()
 
 
 def solution(mesh):
@@ -508,9 +528,9 @@
         out = pl.pallas_call(
             functools.partial(kernel, ngx, ngy),
             out_shape=(
-                jax.ShapeDtypeStruct(temp.shape, F32),
-                jax.ShapeDtypeStruct(wall.shape, F32),
-                jax.ShapeDtypeStruct(stemp.shape, F32),
+                pltpu.VMEM(temp.shape, F32),
+                pltpu.VMEM(wall.shape, F32),
+                pltpu.VMEM(stemp.shape, F32),
             ),
             in_specs=[hbm, hbm, hbm, vmem, pl.BlockSpec(memory_space=pltpu.SMEM), vmem, vmem, vmem, vmem],
             out_specs=(vmem, vmem, vmem),
@@ -543,8 +563,10 @@
                 pltpu.VMEM((ngy, 8, 128), F32),
                 pltpu.VMEM((ngx, 8, 128), F32),
                 pltpu.VMEM((ngx, 8, 128), F32),
-                pltpu.VMEM((ndev, 2, 128), F32),
-                dma((3,)),
+                pltpu.VMEM((ngx, 32, 128), F32),
+                pltpu.VMEM((ngy, 8, 128), F32),
+                pltpu.VMEM((ngy, 8, 128), F32),
+                dma((3, 2)),
                 dma((4, 2)),
                 dma((4, 2)),
                 dma((2, 2)),
@@ -553,17 +575,27 @@
                 dma((2, 2)),
                 dma((2, 2)),
                 dma((2, 2)),
-                dma((5,)),
-                dma((5,)),
-                dma((1,)),
-                pltpu.SemaphoreType.REGULAR((3,)),
+                dma((6,)),
+                dma((6,)),
             ],
             compiler_params=pltpu.CompilerParams(
                 collective_id=0, has_side_effects=True, vmem_limit_bytes=60 << 20
             ),
             name="coupled_step",
         )(temp, kappa, vel, wall, count, fmap.reshape(1, -1), stemp, scond, cool)
-        return out
+        return pl.pallas_call(
+            finish,
+            out_shape=(
+                jax.ShapeDtypeStruct(temp.shape, F32),
+                jax.ShapeDtypeStruct(wall.shape, F32),
+                jax.ShapeDtypeStruct(stemp.shape, F32),
+            ),
+            in_specs=[vmem] * 3,
+            out_specs=(hbm,) * 3,
+            scratch_shapes=[dma((3,))],
+            compiler_params=pltpu.CompilerParams(vmem_limit_bytes=1 << 20),
+            name="write_out",
+        )(*[pltpu.with_memory_space_constraint(o, pltpu.VMEM) for o in out])
 
     return jax.shard_map(
         shards,

time: 51.5 us -> 33.7 us (0.65)
  Pallas kernels: 45.6 us -> 32.2 us
  local copies, waits for them, and re-layouts: 4.42 us -> 0 us
    pallas_call x1 -> x2, Pallas kernels: 45.6 us -> 32.2 us  [the longest x1 30.9 us: shards(): pl.pallas_call(functools.partial(kernel, ngx, ngy), out_shape=(pltpu.VMEM...]
    unnamed x7 -> x0, local copies, waits for them, and re-layouts: 4.42 us -> none
where the time goes in v2:
time: 33.7 us; the launch traced here: 33.5 us
  Pallas kernels  32.2 us (96%)
  between operations  1.29 us (4%)
    pallas_call x1, Pallas kernels, shards(): pl.pallas_call(functools.partial(kernel, ngx, ngy), out_shape=(pltpu.VMEM...  30.9 us
    pallas_call x1, Pallas kernels, shards(): pl.pallas_call(finish, out_shape=(jax.ShapeDtypeStruct(temp.shape, F32),...  1.35 us

profile of v2, /device:TPU:1, one launch (start us, length us, event | category | flops | bytes accessed | tf_op | source)
XLA Modules:
  0.0 33.5 jit_solution(12378315658890459318)
XLA Ops:
  1.3 30.9 %coupled_step.1 = (f32[32,32,512]{2,1,0:T(8,128)S(1)}, f32[32,32]{1,0:T(8,128)S(1)}, f32[2,32,128]{2,1,0:T(8,128)S(1)}) custom-call(f32[32,32,512]{2,1,0:T(8,128)} %t_hbm.1, bf16[32,32,512]{2,1,0:T(8,128)(2,1)} %k_hbm.1, bf16[3,32,32,512]{3,2,1,0:T(8,128)(2,1)} %v_hbm.1, f32[32,32]{1,0:T(8,128)} %wall_ref.1, s32[1]{0:T(128)S(6)} %copy.12.count_ref, ...), custom_call_target="tpu_custom_call" | custom-call | tf_op jit(solution)/shard_map/coupled_step/pallas_call | solution.py:528
  32.2 1.4 %write_out.1 = (f32[32,32,512]{2,1,0:T(8,128)}, f32[32,32]{1,0:T(8,128)}, f32[2,32,128]{2,1,0:T(8,128)}) custom-call(f32[32,32,512]{2,1,0:T(8,128)S(1)} %get-tuple-element.6.fluid, f32[32,32]{1,0:T(8,128)S(1)} %get-tuple-element.7.wall, f32[2,32,128]{2,1,0:T(8,128)S(1)} %get-tuple-element.8.solid), custom_call_target="tpu_custom_call" | custom-call | tf_op jit(solution)/shard_map/write_out/pallas_call | solution.py:586

commit v3 on v2

--- a/solution.py
+++ b/solution.py
@@ -24,6 +24,19 @@
 
 def iota(shape, axis):
     return lax.broadcasted_iota(jnp.int32, shape, axis)
+
+
+def thirds(value):
+    pieces = []
+    for _ in range(3):
+        piece = value.astype(jnp.bfloat16)
+        pieces.append(piece)
+        value = value - piece.astype(F32)
+    return pieces
+
+
+def pick_rows(onehot, pieces):
+    return sum(jnp.dot(onehot, piece, preferred_element_type=F32) for piece in pieces)
 
 
 def slab_step(temp, k0, ux, uy, uz, wall, t_nb, k_nb, u_nb):
@@ -205,12 +218,7 @@
     def slab(value):
         return nt_dot(pick16, value.reshape(cells, 128))
 
-    rest = tp[1 : nx + 1, PAD : PAD + ny, 0:128].reshape(cells, 128)
-    s_t = jnp.zeros((8, cells), F32)
-    for _ in range(3):
-        piece = rest.astype(jnp.bfloat16)
-        s_t = s_t + nt_dot(pick16, piece)
-        rest = rest - piece.astype(F32)
+    s_t = sum(nt_dot(pick16, piece) for piece in thirds(tp[1 : nx + 1, PAD : PAD + ny, 0:128].reshape(cells, 128)))
     s_k = 0.5 * slab(kraw[:, :, 0:128])
     s_ux = 0.25 * slab(vraw[0, :, :, 0:128])
     s_uy = 0.25 * slab(vraw[1, :, :, 0:128])
@@ -225,10 +233,9 @@
         wx_send[up, 4:6, :] = s_ux[0:2, lanes]
         wx_send[up, 6:8, :] = jnp.zeros((2, 128), F32)
     pl.semaphore_wait(barrier, len(peers))
+    spread(lambda k: csend, cbuf, i, ngx, gxd, gs.at[0], gr.at[0])
     wy[0]()
     wx[0]()
-    spread(lambda k: csend, cbuf, i, ngx, gxd, gs.at[0], gr.at[0])
-    spread(lambda k: tops.at[i], tops, i, ngx, gxd, gs.at[4], gr.at[4])
     for load in loads[1]:
         load.wait()
 
@@ -301,6 +308,58 @@
     cc[j, 0:8] = cond_blocks
     cc[j, 8:16] = column
     spread(lambda k: cc.at[j], cc, j, ngy, gyd, gs.at[1], gr.at[1])
+    spread(lambda k: tops.at[i], tops, i, ngx, gxd, gs.at[4], gr.at[4])
+
+    zlane = iota((8, nz), 1)
+    z_first, z_last = zlane == 0, zlane == nz - 1
+
+    def stencil(src, x, yt, co):
+        y0 = PAD + yt
+        mid = src[x + 1, y0 : y0 + 8, :]
+        wall = jnp.concatenate([wallb[x, pl.ds(yt, 8)]] * (nz // 128), axis=1)
+        down = jnp.where(z_first, wall, pltpu.roll(mid, 1, 1))
+        out = co(0) * mid
+        out = out + co(1) * src[x + 2, y0 : y0 + 8, :]
+        out = out + co(2) * src[x, y0 : y0 + 8, :]
+        out = out + co(3) * src[x + 1, y0 + 1 : y0 + 9, :]
+        out = out + co(4) * src[x + 1, y0 - 1 : y0 + 7, :]
+        out = out + co(5) * pltpu.roll(mid, nz - 1, 1)
+        return out + co(6) * down
+
+    def advance_first(x, yt):
+        y0 = PAD + yt
+        k0 = kp[x + 1, y0 : y0 + 8, :]
+        ux0 = uxp[x + 1, yt : yt + 8, :]
+        uy0 = uyp[x, y0 : y0 + 8, :]
+        uz0 = uzp[x, yt : yt + 8, :]
+        kk, uu = k0 + kp[x + 2, y0 : y0 + 8, :], ux0 + uxp[x + 2, yt : yt + 8, :]
+        total, c1 = kk + uu, kk - uu
+        kk, uu = k0 + kp[x, y0 : y0 + 8, :], ux0 + uxp[x, yt : yt + 8, :]
+        total, c2 = total + (kk - uu), kk + uu
+        kk, uu = k0 + kp[x + 1, y0 + 1 : y0 + 9, :], uy0 + uyp[x, y0 + 1 : y0 + 9, :]
+        total, c3 = total + (kk + uu), kk - uu
+        kk, uu = k0 + kp[x + 1, y0 - 1 : y0 + 7, :], uy0 + uyp[x, y0 - 1 : y0 + 7, :]
+        total, c4 = total + (kk - uu), kk + uu
+        low, high = k0 - uz0, k0 + uz0
+        c5 = jnp.where(z_last, 0.0, low + pltpu.roll(low, nz - 1, 1))
+        total = total + (high + jnp.where(z_last, 0.0, pltpu.roll(high, nz - 1, 1)))
+        c6 = high + jnp.where(z_first, 0.0, pltpu.roll(high, 1, 1))
+        total = total + (low + jnp.where(z_first, 0.0, pltpu.roll(low, 1, 1)))
+        made = (1.0 - total, c1, c2, c3, c4, c5, c6)
+        for n, value in enumerate(made):
+            coef[n, x, pl.ds(yt, 8)] = value
+        value = stencil(tp, x, yt, lambda n: made[n])
+        t1p[x + 1, y0 : y0 + 8, :] = value
+        return value
+
+    middle = range(8, ny - 8, 8)
+
+    def middle_body(x, carry):
+        for yt in middle:
+            advance_first(x, yt)
+        return carry
+
+    lax.fori_loop(1, nx - 1, middle_body, 0, unroll=5)
 
     vy[1]()
     vx[1]()
@@ -313,75 +372,20 @@
     ys[1]()
     xk[1]()
     xu[1]()
-    zlane = iota((8, nz), 1)
-    z_first, z_last = zlane == 0, zlane == nz - 1
-
-    def coef_body(x, carry):
-        kp[x + 1, PAD - 1 : PAD, :] = ys_recv[0, 1, x]
-        kp[x + 1, PAD + ny : PAD + ny + 1, :] = ys_recv[1, 1, x]
-        uyp[x, PAD - 1 : PAD, :] = ys_recv[0, 2, x]
-        uyp[x, PAD + ny : PAD + ny + 1, :] = ys_recv[1, 2, x]
-        tp[x + 1, PAD - 1 : PAD, :] = ys_recv[0, 0, x]
-        tp[x + 1, PAD + ny : PAD + ny + 1, :] = ys_recv[1, 0, x]
-        for yt in range(0, ny, 8):
-            y0 = PAD + yt
-            k0 = kp[x + 1, y0 : y0 + 8, :]
-            ux0 = uxp[x + 1, yt : yt + 8, :]
-            uy0 = uyp[x, y0 : y0 + 8, :]
-            uz0 = uzp[x, yt : yt + 8, :]
-            here = pl.ds(yt, 8)
-            kk, uu = k0 + kp[x + 2, y0 : y0 + 8, :], ux0 + uxp[x + 2, yt : yt + 8, :]
-            coef[1, x, here] = kk - uu
-            total = kk + uu
-            kk, uu = k0 + kp[x, y0 : y0 + 8, :], ux0 + uxp[x, yt : yt + 8, :]
-            coef[2, x, here] = kk + uu
-            total = total + (kk - uu)
-            kk, uu = k0 + kp[x + 1, y0 + 1 : y0 + 9, :], uy0 + uyp[x, y0 + 1 : y0 + 9, :]
-            coef[3, x, here] = kk - uu
-            total = total + (kk + uu)
-            kk, uu = k0 + kp[x + 1, y0 - 1 : y0 + 7, :], uy0 + uyp[x, y0 - 1 : y0 + 7, :]
-            coef[4, x, here] = kk + uu
-            total = total + (kk - uu)
-            kk = k0 + jnp.where(z_last, 0.0, pltpu.roll(k0, nz - 1, 1))
-            uu = uz0 + jnp.where(z_last, 0.0, pltpu.roll(uz0, nz - 1, 1))
-            coef[5, x, here] = jnp.where(z_last, 0.0, kk - uu)
-            total = total + (kk + uu)
-            kk = k0 + jnp.where(z_first, 0.0, pltpu.roll(k0, 1, 1))
-            uu = uz0 + jnp.where(z_first, 0.0, pltpu.roll(uz0, 1, 1))
-            coef[6, x, here] = kk + uu
-            total = total + (kk - uu)
-            coef[0, x, here] = 1.0 - total
+    xt[1]()
+    for x in (0, nx - 1):
+        middle_body(x, 0)
+
+    def edge_body(x, carry):
+        for row, side in ((PAD - 1, 0), (PAD + ny, 1)):
+            tp[x + 1, row : row + 1, :] = ys_recv[side, 0, x]
+            kp[x + 1, row : row + 1, :] = ys_recv[side, 1, x]
+            uyp[x, row : row + 1, :] = ys_recv[side, 2, x]
+        y1_send[0, x] = advance_first(x, 0)[0:1]
+        y1_send[1, x] = advance_first(x, ny - 8)[7:8]
         return carry
 
-    lax.fori_loop(0, nx, coef_body, 0, unroll=4)
-
-    def step_at(src, x, yt):
-        y0 = PAD + yt
-        here = pl.ds(yt, 8)
-        mid = src[x + 1, y0 : y0 + 8, :]
-        wall = jnp.concatenate([wallb[x, here]] * (nz // 128), axis=1)
-        down = jnp.where(z_first, wall, pltpu.roll(mid, 1, 1))
-        out = coef[0, x, here] * mid
-        out = out + coef[1, x, here] * src[x + 2, y0 : y0 + 8, :]
-        out = out + coef[2, x, here] * src[x, y0 : y0 + 8, :]
-        out = out + coef[3, x, here] * src[x + 1, y0 + 1 : y0 + 9, :]
-        out = out + coef[4, x, here] * src[x + 1, y0 - 1 : y0 + 7, :]
-        out = out + coef[5, x, here] * pltpu.roll(mid, nz - 1, 1)
-        return out + coef[6, x, here] * down
-
-    xt[1]()
-
-    def first_body(x, carry):
-        for yt in range(0, ny, 8):
-            value = step_at(tp, x, yt)
-            t1p[x + 1, PAD + yt : PAD + yt + 8, :] = value
-            if yt == 0:
-                y1_send[0, x] = value[0:1]
-            if yt == ny - 8:
-                y1_send[1, x] = value[7:8]
-        return carry
-
-    lax.fori_loop(0, nx, first_body, 0, unroll=4)
+    lax.fori_loop(0, nx, edge_body, 0, unroll=4)
     y1[0]()
     x1[0]()
 
@@ -410,34 +414,35 @@
     owner = 2 * ((line // 8) * ngy + j)
     for_near = jnp.where(kind < 2, owner + kind, -2).astype(F32)
     for_cond = jnp.where((kind >= 2) & (kind < 4), owner + kind - 2, -2).astype(F32)
-    w_near = (for_near == target).astype(F32)
-    w_cond = (for_cond == target).astype(F32)
-    cond_rows = cc[:, 0:8].reshape(128, 128)
-    payload_c = jnp.dot(w_cond, cond_rows, precision=EXACT, preferred_element_type=F32)
+    w_near = (for_near == target).astype(F32).astype(jnp.bfloat16)
+    w_cond = (for_cond == target).astype(F32).astype(jnp.bfloat16)
+    cond_rows = thirds(cc[:, 0:8].reshape(128, 128))
+    payload_c = pick_rows(w_cond, cond_rows)
 
     top_line = iota((128, 128), 0)
     top_row = lax.rem(top_line, 8)
     top_block = top_line // 8
     top_id = jnp.where(top_row == 0, 2 * ((top_block // 2) * ngy + j) + lax.rem(top_block, 2), -2)
     w_top = (top_id.astype(F32) == target).astype(F32)
-    w_back = jnp.transpose(w_top)
+    w_back = jnp.transpose(w_top).astype(jnp.bfloat16)
+    w_top = w_top.astype(jnp.bfloat16)
     all_in(tops, ngx, gr.at[4])
     top_t = tops[:, 0:16].reshape(128, 128)
     top_c = tops[:, 16:32].reshape(128, 128)
     top_up, top_dn, top_lf, top_rt = conductances(top_c, 8)
-    top_bound = WALL_RATIO * jnp.dot(w_top, cond_rows, precision=EXACT, preferred_element_type=F32)
+    top_bound = WALL_RATIO * pick_rows(w_top, cond_rows)
     top_inv = 1.0 / (top_up + top_dn + top_lf + top_rt + top_bound)
 
     all_in(nb, ngy, gr.at[2])
-    near_rows = nb[...].reshape(128, 128)
-    payload = payload_c + jnp.dot(w_near, near_rows, precision=EXACT, preferred_element_type=F32)
+    near_rows = thirds(nb[...].reshape(128, 128))
+    payload = payload_c + pick_rows(w_near, near_rows)
     m3s[...] = payload.reshape(ngx, 8, 128)
     spread(lambda k: m3s.at[gxd(k)[0]], m3r, i, ngx, gxd, gs.at[3], gr.at[3])
     m3r[i] = m3s[i]
-    top_src = top_bound * jnp.dot(w_top, near_rows, precision=EXACT, preferred_element_type=F32)
+    top_src = top_bound * pick_rows(w_top, near_rows)
     for _ in range(SWEEPS):
         top_t = sweep(top_t, top_up, top_dn, top_lf, top_rt, top_src, top_inv)
-    m5s[...] = jnp.dot(w_back, top_t, precision=EXACT, preferred_element_type=F32).reshape(ngy, 8, 128)
+    m5s[...] = pick_rows(w_back, thirds(top_t)).reshape(ngy, 8, 128)
     spread(lambda k: m5s.at[gyd(k)[1]], m5r, j, ngy, gyd, gs.at[5], gr.at[5])
     m5r[j] = m5s[j]
 
@@ -454,6 +459,18 @@
         )
 
     cool_at = per_block(cool[0:1], cool[1:2])
+
+    y1[1]()
+    x1[1]()
+
+    def second_body(x, carry):
+        t1p[x + 1, PAD - 1 : PAD, :] = y1_recv[0, x]
+        t1p[x + 1, PAD + ny : PAD + ny + 1, :] = y1_recv[1, x]
+        for yt in range(0, ny, 8):
+            fluid_ref[x, pl.ds(yt, 8)] = stencil(t1p, x, yt, lambda n: coef[n, x, pl.ds(yt, 8)])
+        return carry
+
+    lax.fori_loop(0, nx, second_body, 0, unroll=4)
 
     all_in(m3r, ngx, gr.at[3])
     arrived = m3r[0]
@@ -468,18 +485,6 @@
     for _ in range(SWEEPS):
         temps = sweep(temps, c_up, c_dn, c_lf, c_rt, source, inverse)
     solid_ref[...] = temps.reshape(2, layers, width)
-
-    y1[1]()
-    x1[1]()
-
-    def second_body(x, carry):
-        t1p[x + 1, PAD - 1 : PAD, :] = y1_recv[0, x]
-        t1p[x + 1, PAD + ny : PAD + ny + 1, :] = y1_recv[1, x]
-        for yt in range(0, ny, 8):
-            fluid_ref[x, pl.ds(yt, 8)] = step_at(t1p, x, yt)
-        return carry
-
-    lax.fori_loop(0, nx, second_body, 0, unroll=4)
 
     for group in (wy, wx, vy, vx, ys, xt, xk, xu, y1, x1):
         group[2]()

time: 33.7 us -> 31.5 us (0.935)
  Pallas kernels: 32.2 us -> 30 us
    pallas_call x1, Pallas kernels: 30.9 us -> 28.7 us  [shards(): pl.pallas_call(functools.partial(kernel, ngx, ngy), out_shape=(pltpu.VMEM...]
where the time goes in v3:
time: 31.5 us; the launch traced here: 31.3 us
  Pallas kernels  30 us (95%)
  between operations  1.29 us (4%)
    pallas_call x1, Pallas kernels, shards(): pl.pallas_call(functools.partial(kernel, ngx, ngy), out_shape=(pltpu.VMEM...  28.7 us
    pallas_call x1, Pallas kernels, shards(): pl.pallas_call(finish, out_shape=(jax.ShapeDtypeStruct(temp.shape, F32),...  1.35 us

profile of v3, /device:TPU:1, one launch (start us, length us, event | category | flops | bytes accessed | tf_op | source)
XLA Modules:
  0.0 31.3 jit_solution(16798425068457355600)
XLA Ops:
  1.3 28.7 %coupled_step.1 = (f32[32,32,512]{2,1,0:T(8,128)S(1)}, f32[32,32]{1,0:T(8,128)S(1)}, f32[2,32,128]{2,1,0:T(8,128)S(1)}) custom-call(f32[32,32,512]{2,1,0:T(8,128)} %t_hbm.1, bf16[32,32,512]{2,1,0:T(8,128)(2,1)} %k_hbm.1, bf16[3,32,32,512]{3,2,1,0:T(8,128)(2,1)} %v_hbm.1, f32[32,32]{1,0:T(8,128)} %wall_ref.1, s32[1]{0:T(128)S(6)} %copy.12.count_ref, ...), custom_call_target="tpu_custom_call" | custom-call | tf_op jit(solution)/shard_map/coupled_step/pallas_call | solution.py:533
  29.9 1.4 %write_out.1 = (f32[32,32,512]{2,1,0:T(8,128)}, f32[32,32]{1,0:T(8,128)}, f32[2,32,128]{2,1,0:T(8,128)}) custom-call(f32[32,32,512]{2,1,0:T(8,128)S(1)} %get-tuple-element.6.fluid, f32[32,32]{1,0:T(8,128)S(1)} %get-tuple-element.7.wall, f32[2,32,128]{2,1,0:T(8,128)S(1)} %get-tuple-element.8.solid), custom_call_target="tpu_custom_call" | custom-call | tf_op jit(solution)/shard_map/write_out/pallas_call | solution.py:591

commit v4 on v3

--- a/solution.py
+++ b/solution.py
@@ -39,21 +39,22 @@
     return sum(jnp.dot(onehot, piece, preferred_element_type=F32) for piece in pieces)
 
 
-def slab_step(temp, k0, ux, uy, uz, wall, t_nb, k_nb, u_nb):
+def across(temp, k0, own, n, kn, un, sign):
+    return (k0 + kn) * (n - temp) - sign * (own + un) * (temp + n)
+
+
+def upright(temp, k0, uz, wall):
     rows = temp.shape[0]
-    row = iota(temp.shape, 0)
-    out = temp
-    for pos, (sign, own) in enumerate(((1, ux), (-1, ux), (1, uy), (-1, uy))):
-        kk, uu, n = k0 + k_nb[pos], own + u_nb[pos], t_nb[pos]
-        out = out + kk * (n - temp) - sign * uu * (temp + n)
-    up = pltpu.roll(temp, rows - 1, 0)
-    kk, uu = k0 + pltpu.roll(k0, rows - 1, 0), uz + pltpu.roll(uz, rows - 1, 0)
-    out = out + kk * (up - temp) - uu * (temp + up)
-    first = row == 0
-    down = jnp.where(first, wall, pltpu.roll(temp, 1, 0))
-    kk = k0 + jnp.where(first, 0.0, pltpu.roll(k0, 1, 0))
-    uu = uz + jnp.where(first, 0.0, pltpu.roll(uz, 1, 0))
-    return out + kk * (down - temp) + uu * (temp + down)
+    first = iota(temp.shape, 0) == 0
+
+    def above(value):
+        return pltpu.roll(value, rows - 1, 0)
+
+    def below(value, ground):
+        return jnp.where(first, ground, pltpu.roll(value, 1, 0))
+
+    out = temp + across(temp, k0, uz, above(temp), above(k0), above(uz), 1.0)
+    return out + across(temp, k0, uz, below(temp, wall), below(k0, 0.0), below(uz, 0.0), -1.0)
 
 
 def conductances(conds, layers):
@@ -79,9 +80,9 @@
     fluid_ref, wallout_ref, solid_ref,
     tp, t1p, kp, uxp, uyp, uzp, coef, kraw, vraw, wallb,
     ys_send, ys_recv, y1_send, y1_recv,
-    wy_send, wy_recv, wx_send, wx_recv, vy_send, vy_recv, vx_send, vx_recv,
+    wy_send, wy_recv, wx_send, wx_recv, wd_recv,
     cbuf, csend, cc, nb, m3s, m3r, tops, m5s, m5r,
-    ld_sem, hs, hr, t1s, t1r, ws, wr, v2s, v2r, gs, gr,
+    ld_sem, hs, hr, t1s, t1r, ws, wr, wds, wdr, gs, gr,
 ):
     nx, ny, nz = t_hbm.shape
     cells = nx * ny
@@ -99,6 +100,7 @@
 
     barrier = pltpu.get_barrier_semaphore()
     peers = [gxd(k) for k in range(1, ngx)] + [gyd(k) for k in range(1, ngy)]
+    peers += [(gxd(dx)[0], gyd(dy)[1]) for dx in (1, -1) for dy in (1, -1)]
     for peer in peers:
         pl.semaphore_signal(barrier, inc=1, device_id=peer, device_id_type=MESH)
     loads = []
@@ -133,7 +135,7 @@
             uxp[plane] = jnp.zeros(uxp.shape[1:], F32)
             side = 0 if plane == 0 else 1
             wx_recv[side] = jnp.zeros(wx_recv.shape[1:], F32)
-            vx_recv[side] = jnp.zeros(vx_recv.shape[1:], F32)
+            wd_recv[side] = jnp.zeros(wd_recv.shape[1:], F32)
 
     for cond, side in ((j == 0, 0), (j == ngy - 1, 1)):
 
@@ -142,7 +144,7 @@
             ys_recv[side] = jnp.zeros(ys_recv.shape[1:], F32)
             y1_recv[side] = jnp.zeros(y1_recv.shape[1:], F32)
             wy_recv[side] = jnp.zeros(wy_recv.shape[1:], F32)
-            vy_recv[side] = jnp.zeros(vy_recv.shape[1:], F32)
+            wd_recv[:, side] = jnp.zeros((2, 8, 128), F32)
 
     s_w = jnp.concatenate([wall_ref[x : x + 1, :] for x in range(nx)], axis=1)
 
@@ -176,8 +178,18 @@
 
     wy = halo(lambda up: wy_send, lambda up: wy_recv.at[1 - up], ws.at[0], wr.at[0], 1)
     wx = halo(lambda up: wx_send.at[up], lambda up: wx_recv.at[1 - up], ws.at[1], wr.at[1], 0)
-    vy = halo(lambda up: vy_send, lambda up: vy_recv.at[1 - up], v2s.at[0], v2r.at[0], 1)
-    vx = halo(lambda up: vx_send.at[up], lambda up: vx_recv.at[1 - up], v2s.at[1], v2r.at[1], 0)
+    corners = []
+    for upx in (0, 1):
+        for upy in (0, 1):
+            copy = pltpu.make_async_remote_copy(
+                src_ref=wx_send.at[upx], dst_ref=wd_recv.at[1 - upx, 1 - upy],
+                send_sem=wds.at[upx, upy], recv_sem=wdr.at[upx, upy],
+                device_id=(gxd(1 if upx else -1)[0], gyd(1 if upy else -1)[1]), device_id_type=MESH,
+            )
+            low_x, high_x, low_y, high_y = i > 0, i < ngx - 1, j > 0, j < ngy - 1
+            sends = jnp.logical_and(high_x if upx else low_x, high_y if upy else low_y)
+            gets = jnp.logical_and(low_x if upx else high_x, low_y if upy else high_y)
+            corners.append((copy, sends, gets))
     ys = halo(lambda up: ys_send.at[up], lambda up: ys_recv.at[1 - up], hs.at[0], hr.at[0], 1)
 
     def planes(ref, padded):
@@ -223,19 +235,29 @@
     s_ux = 0.25 * slab(vraw[0, :, :, 0:128])
     s_uy = 0.25 * slab(vraw[1, :, :, 0:128])
     s_uz = 0.25 * slab(vraw[2, :, :, 0:128])
-    wy_send[0:2, :] = s_t[0:2]
-    wy_send[2:4, :] = s_k[0:2]
-    wy_send[4:6, :] = s_uy[0:2]
-    wy_send[6:8, :] = jnp.zeros((2, cells), F32)
+    lane = iota((8, cells), 1)
+    y_first, y_last = lax.rem(lane, ny) == 0, lax.rem(lane, ny) == ny - 1
+    x_first, x_last = lane < ny, lane >= cells - ny
+    partial = upright(s_t, s_k, s_uz, s_w)
+    for shift, edge, own, sign in (
+        (cells - ny, x_last, s_ux, 1.0), (ny, x_first, s_ux, -1.0),
+        (cells - 1, y_last, s_uy, 1.0), (1, y_first, s_uy, -1.0),
+    ):
+        term = across(
+            s_t, s_k, own, pltpu.roll(s_t, shift, 1), pltpu.roll(s_k, shift, 1), pltpu.roll(own, shift, 1), sign
+        )
+        partial = partial + jnp.where(edge, 0.0, term)
+    wy_send[...] = jnp.concatenate([s_t[0:2], s_k[0:2], s_uy[0:2], partial[0:1], s_ux[0:1]], axis=0)
     for up, lanes in ((1, slice(cells - 128, cells)), (0, slice(0, 128))):
-        wx_send[up, 0:2, :] = s_t[0:2, lanes]
-        wx_send[up, 2:4, :] = s_k[0:2, lanes]
-        wx_send[up, 4:6, :] = s_ux[0:2, lanes]
-        wx_send[up, 6:8, :] = jnp.zeros((2, 128), F32)
+        wx_send[up] = jnp.concatenate(
+            [s_t[0:2, lanes], s_k[0:2, lanes], s_ux[0:2, lanes], partial[0:1, lanes], s_uy[0:1, lanes]], axis=0
+        )
     pl.semaphore_wait(barrier, len(peers))
     spread(lambda k: csend, cbuf, i, ngx, gxd, gs.at[0], gr.at[0])
     wy[0]()
     wx[0]()
+    for copy, sends, gets in corners:
+        pl.when(sends)(copy.start)
     for load in loads[1]:
         load.wait()
 
@@ -259,56 +281,6 @@
     xk[0]()
     xu[0]()
     xt[0]()
-
-    lane = iota((8, cells), 1)
-    y_first, y_last = lax.rem(lane, ny) == 0, lax.rem(lane, ny) == ny - 1
-    x_first, x_last = lane < ny, lane >= cells - ny
-
-    def y_neighbours(own, low, high):
-        plus = jnp.where(y_last, pltpu.roll(high, ny - 1, 1), pltpu.roll(own, cells - 1, 1))
-        minus = jnp.where(y_first, pltpu.roll(low, cells - (ny - 1), 1), pltpu.roll(own, 1, 1))
-        return plus, minus
-
-    def widen(tile):
-        return jnp.concatenate([tile] * (cells // 128), axis=1)
-
-    def x_neighbours(own, low, high):
-        plus = jnp.where(x_last, widen(pltpu.roll(high, 128 - ny, 1)), pltpu.roll(own, cells - ny, 1))
-        minus = jnp.where(x_first, widen(pltpu.roll(low, ny, 1)), pltpu.roll(own, ny, 1))
-        return plus, minus
-
-    wy[1]()
-    wx[1]()
-
-    def rows_of(value, part):
-        return pltpu.roll(value, 8 - 2 * part, 0) if part else value
-
-    ylow, yhigh, xlow, xhigh = wy_recv[0], wy_recv[1], wx_recv[0], wx_recv[1]
-    ty = y_neighbours(s_t, rows_of(ylow, 0), rows_of(yhigh, 0))
-    ky = y_neighbours(s_k, rows_of(ylow, 1), rows_of(yhigh, 1))
-    uy = y_neighbours(s_uy, rows_of(ylow, 2), rows_of(yhigh, 2))
-    tx = x_neighbours(s_t, rows_of(xlow, 0), rows_of(xhigh, 0))
-    kx = x_neighbours(s_k, rows_of(xlow, 1), rows_of(xhigh, 1))
-    ux = x_neighbours(s_ux, rows_of(xlow, 2), rows_of(xhigh, 2))
-    k_nb, u_nb = kx + ky, ux + uy
-    first = slab_step(s_t, s_k, s_ux, s_uy, s_uz, s_w, tx + ty, k_nb, u_nb)
-    vy_send[...] = first
-    vx_send[1] = first[:, cells - 128 :]
-    vx_send[0] = first[:, 0:128]
-    vy[0]()
-    vx[0]()
-
-    cbuf[i] = counts
-    cond_blocks = jnp.concatenate([s_k[0:1, 128 * b : 128 * b + 128] for b in range(nblk)], axis=0)
-    all_in(cbuf, ngx, gr.at[0])
-    row8 = iota((8, 128), 0)
-    column = jnp.zeros((8, 128), F32)
-    for k in range(ngx):
-        column = column + jnp.where(row8 == k, cbuf[k], 0.0)
-    cc[j, 0:8] = cond_blocks
-    cc[j, 8:16] = column
-    spread(lambda k: cc.at[j], cc, j, ngy, gyd, gs.at[1], gr.at[1])
-    spread(lambda k: tops.at[i], tops, i, ngx, gxd, gs.at[4], gr.at[4])
 
     zlane = iota((8, nz), 1)
     z_first, z_last = zlane == 0, zlane == nz - 1
@@ -361,11 +333,59 @@
 
     lax.fori_loop(1, nx - 1, middle_body, 0, unroll=5)
 
-    vy[1]()
-    vx[1]()
-    ty = y_neighbours(first, vy_recv[0], vy_recv[1])
-    tx = x_neighbours(first, vx_recv[0], vx_recv[1])
-    second = slab_step(first, s_k, s_ux, s_uy, s_uz, s_w, tx + ty, k_nb, u_nb)
+    cbuf[i] = counts
+    cond_blocks = jnp.concatenate([s_k[0:1, 128 * b : 128 * b + 128] for b in range(nblk)], axis=0)
+    all_in(cbuf, ngx, gr.at[0])
+    row8 = iota((8, 128), 0)
+    column = jnp.zeros((8, 128), F32)
+    for k in range(ngx):
+        column = column + jnp.where(row8 == k, cbuf[k], 0.0)
+    cc[j, 0:8] = cond_blocks
+    cc[j, 8:16] = column
+    spread(lambda k: cc.at[j], cc, j, ngy, gyd, gs.at[1], gr.at[1])
+    spread(lambda k: tops.at[i], tops, i, ngx, gxd, gs.at[4], gr.at[4])
+
+    def widen(tile):
+        return jnp.concatenate([tile] * (cells // 128), axis=1)
+
+    def row_first(value, row):
+        return pltpu.roll(value, 8 - row, 0) if row else value
+
+    wy[1]()
+    wx[1]()
+    for copy, sends, gets in corners:
+        pl.when(gets)(copy.wait_recv)
+    diag = {
+        (sx, sy): pltpu.roll(wd_recv[sx, sy], shift, 1)
+        for sx, sy, shift in ((0, 0, 1), (1, 0, 128 - ny + 1 - ny), (0, 1, 2 * ny - 1), (1, 1, 127))
+    }
+    first = partial
+    beside = []
+    for edge, seen, own, shift, sign, along, side, there in (
+        (x_last, widen(pltpu.roll(wx_recv[1], 128 - ny, 1)), s_ux, cells - ny, 1.0, "x", 1, i < ngx - 1),
+        (x_first, widen(pltpu.roll(wx_recv[0], ny, 1)), s_ux, ny, -1.0, "x", 0, i > 0),
+        (y_last, pltpu.roll(wy_recv[1], ny - 1, 1), s_uy, cells - 1, 1.0, "y", 1, j < ngy - 1),
+        (y_first, pltpu.roll(wy_recv[0], cells - (ny - 1), 1), s_uy, 1, -1.0, "y", 0, j > 0),
+    ):
+        n, kn, un = seen, row_first(seen, 2), row_first(seen, 4)
+        term = across(s_t, s_k, own, n, kn, un, sign)
+        first = first + jnp.where(edge, term, 0.0)
+        beyond = row_first(seen, 6) - term
+        cross = row_first(seen, 7)
+        for other in (0, 1):
+            d = widen(diag[(side, other)] if along == "x" else diag[(other, side)])
+            ends = (y_last if other else y_first) if along == "x" else (x_last if other else x_first)
+            d_u = row_first(d, 7 if along == "x" else 4)
+            corner = across(n, kn, cross, d, row_first(d, 2), d_u, 1.0 if other else -1.0)
+            beyond = beyond + jnp.where(ends, corner, 0.0)
+        beyond = beyond * there.astype(F32)
+        k_side = jnp.where(edge, kn, pltpu.roll(s_k, shift, 1))
+        u_side = jnp.where(edge, un, pltpu.roll(own, shift, 1))
+        beside.append((edge, beyond, own, shift, sign, k_side, u_side))
+    second = upright(first, s_k, s_uz, s_w)
+    for edge, beyond, own, shift, sign, k_side, u_side in beside:
+        n = jnp.where(edge, beyond, pltpu.roll(first, shift, 1))
+        second = second + across(first, s_k, own, n, k_side, u_side, sign)
     nb[j] = jnp.concatenate([second[0:1, 128 * b : 128 * b + 128] for b in range(nblk)], axis=0)
     spread(lambda k: nb.at[j], nb, j, ngy, gyd, gs.at[2], gr.at[2])
 
@@ -486,8 +506,10 @@
         temps = sweep(temps, c_up, c_dn, c_lf, c_rt, source, inverse)
     solid_ref[...] = temps.reshape(2, layers, width)
 
-    for group in (wy, wx, vy, vx, ys, xt, xk, xu, y1, x1):
+    for group in (wy, wx, ys, xt, xk, xu, y1, x1):
         group[2]()
+    for copy, sends, gets in corners:
+        pl.when(sends)(copy.wait_send)
     all_in(cbuf, ngx, gs.at[0])
     all_in(cc, ngy, gs.at[1])
     all_in(nb, ngy, gs.at[2])
@@ -558,10 +580,7 @@
                 pltpu.VMEM((2, 8, cells), F32),
                 pltpu.VMEM((2, 8, 128), F32),
                 pltpu.VMEM((2, 8, 128), F32),
-                pltpu.VMEM((8, cells), F32),
-                pltpu.VMEM((2, 8, cells), F32),
-                pltpu.VMEM((2, 8, 128), F32),
-                pltpu.VMEM((2, 8, 128), F32),
+                pltpu.VMEM((2, 2, 8, 128), F32),
                 pltpu.VMEM((ngx, 8, 128), F32),
                 pltpu.VMEM((8, 128), F32),
                 pltpu.VMEM((ngy, 16, 128), F32),

time: 31.5 us -> 29.8 us (0.946)
  Pallas kernels: 30 us -> 28.3 us
    pallas_call x1, Pallas kernels: 28.7 us -> 27 us  [shards(): pl.pallas_call(functools.partial(kernel, ngx, ngy), out_shape=(pltpu.VMEM...]
where the time goes in v4:
time: 29.8 us; the launch traced here: 29.6 us
  Pallas kernels  28.3 us (95%)
  between operations  1.29 us (4%)
    pallas_call x1, Pallas kernels, shards(): pl.pallas_call(functools.partial(kernel, ngx, ngy), out_shape=(pltpu.VMEM...  27 us
    pallas_call x1, Pallas kernels, shards(): pl.pallas_call(finish, out_shape=(jax.ShapeDtypeStruct(temp.shape, F32),...  1.35 us

profile of v4, /device:TPU:1, one launch (start us, length us, event | category | flops | bytes accessed | tf_op | source)
XLA Modules:
  0.0 29.6 jit_solution(16242213109259927273)
XLA Ops:
  1.3 27.0 %coupled_step.1 = (f32[32,32,512]{2,1,0:T(8,128)S(1)}, f32[32,32]{1,0:T(8,128)S(1)}, f32[2,32,128]{2,1,0:T(8,128)S(1)}) custom-call(f32[32,32,512]{2,1,0:T(8,128)} %t_hbm.1, bf16[32,32,512]{2,1,0:T(8,128)(2,1)} %k_hbm.1, bf16[3,32,32,512]{3,2,1,0:T(8,128)(2,1)} %v_hbm.1, f32[32,32]{1,0:T(8,128)} %wall_ref.1, s32[1]{0:T(128)S(6)} %copy.12.count_ref, ...), custom_call_target="tpu_custom_call" | custom-call | tf_op jit(solution)/shard_map/coupled_step/pallas_call | solution.py:555
  28.3 1.4 %write_out.1 = (f32[32,32,512]{2,1,0:T(8,128)}, f32[32,32]{1,0:T(8,128)}, f32[2,32,128]{2,1,0:T(8,128)}) custom-call(f32[32,32,512]{2,1,0:T(8,128)S(1)} %get-tuple-element.6.fluid, f32[32,32]{1,0:T(8,128)S(1)} %get-tuple-element.7.wall, f32[2,32,128]{2,1,0:T(8,128)S(1)} %get-tuple-element.8.solid), custom_call_target="tpu_custom_call" | custom-call | tf_op jit(solution)/shard_map/write_out/pallas_call | solution.py:610

commit v5 on v4

--- a/solution.py
+++ b/solution.py
@@ -35,8 +35,12 @@
     return pieces
 
 
-def pick_rows(onehot, pieces):
-    return sum(jnp.dot(onehot, piece, preferred_element_type=F32) for piece in pieces)
+def thrice(onehot):
+    return jnp.concatenate([onehot.astype(F32).astype(jnp.bfloat16)] * 3, axis=1)
+
+
+def pick_rows(onehot3, value):
+    return jnp.dot(onehot3, jnp.concatenate(thirds(value), axis=0), preferred_element_type=F32)
 
 
 def across(temp, k0, own, n, kn, un, sign):
@@ -79,7 +83,7 @@
     t_hbm, k_hbm, v_hbm, wall_ref, count_ref, map_ref, st_ref, sc_ref, cool_ref,
     fluid_ref, wallout_ref, solid_ref,
     tp, t1p, kp, uxp, uyp, uzp, coef, kraw, vraw, wallb,
-    ys_send, ys_recv, y1_send, y1_recv,
+    ys_send, ys_recv, yh_send, yh_recv, y1_send, y1_recv,
     wy_send, wy_recv, wx_send, wx_recv, wd_recv,
     cbuf, csend, cc, nb, m3s, m3r, tops, m5s, m5r,
     ld_sem, hs, hr, t1s, t1r, ws, wr, wds, wdr, gs, gr,
@@ -142,6 +146,7 @@
         @pl.when(cond)
         def _():
             ys_recv[side] = jnp.zeros(ys_recv.shape[1:], F32)
+            yh_recv[side] = jnp.zeros(yh_recv.shape[1:], jnp.bfloat16)
             y1_recv[side] = jnp.zeros(y1_recv.shape[1:], F32)
             wy_recv[side] = jnp.zeros(wy_recv.shape[1:], F32)
             wd_recv[:, side] = jnp.zeros((2, 8, 128), F32)
@@ -190,7 +195,8 @@
             sends = jnp.logical_and(high_x if upx else low_x, high_y if upy else low_y)
             gets = jnp.logical_and(low_x if upx else high_x, low_y if upy else high_y)
             corners.append((copy, sends, gets))
-    ys = halo(lambda up: ys_send.at[up], lambda up: ys_recv.at[1 - up], hs.at[0], hr.at[0], 1)
+    ys = halo(lambda up: ys_send.at[up, 0], lambda up: ys_recv.at[1 - up, 0], hs.at[0], hr.at[0], 1)
+    yh = halo(lambda up: yh_send.at[up], lambda up: yh_recv.at[1 - up], hs.at[4], hr.at[4], 1)
 
     def planes(ref, padded):
         rows = pl.ds(PAD, ny) if padded else pl.ds(0, ny)
@@ -277,10 +283,15 @@
         return carry
 
     lax.fori_loop(0, nx, convert, 0, unroll=4)
+    for side in (0, 1):
+        for part in (0, 1):
+            yh_send[side, part] = ys_send[side, 1 + part, :, 0, :].astype(jnp.bfloat16)
+    yh[0]()
     ys[0]()
     xk[0]()
     xu[0]()
     xt[0]()
+    spread(lambda k: tops.at[i], tops, i, ngx, gxd, gs.at[4], gr.at[4])
 
     zlane = iota((8, nz), 1)
     z_first, z_last = zlane == 0, zlane == nz - 1
@@ -343,7 +354,6 @@
     cc[j, 0:8] = cond_blocks
     cc[j, 8:16] = column
     spread(lambda k: cc.at[j], cc, j, ngy, gyd, gs.at[1], gr.at[1])
-    spread(lambda k: tops.at[i], tops, i, ngx, gxd, gs.at[4], gr.at[4])
 
     def widen(tile):
         return jnp.concatenate([tile] * (cells // 128), axis=1)
@@ -389,6 +399,10 @@
     nb[j] = jnp.concatenate([second[0:1, 128 * b : 128 * b + 128] for b in range(nblk)], axis=0)
     spread(lambda k: nb.at[j], nb, j, ngy, gyd, gs.at[2], gr.at[2])
 
+    yh[1]()
+    for side in (0, 1):
+        for part in (0, 1):
+            ys_recv[side, 1 + part, :, 0, :] = yh_recv[side, part].astype(F32)
     ys[1]()
     xk[1]()
     xu[1]()
@@ -434,35 +448,37 @@
     owner = 2 * ((line // 8) * ngy + j)
     for_near = jnp.where(kind < 2, owner + kind, -2).astype(F32)
     for_cond = jnp.where((kind >= 2) & (kind < 4), owner + kind - 2, -2).astype(F32)
-    w_near = (for_near == target).astype(F32).astype(jnp.bfloat16)
-    w_cond = (for_cond == target).astype(F32).astype(jnp.bfloat16)
-    cond_rows = thirds(cc[:, 0:8].reshape(128, 128))
-    payload_c = pick_rows(w_cond, cond_rows)
-
     top_line = iota((128, 128), 0)
     top_row = lax.rem(top_line, 8)
     top_block = top_line // 8
     top_id = jnp.where(top_row == 0, 2 * ((top_block // 2) * ngy + j) + lax.rem(top_block, 2), -2)
     w_top = (top_id.astype(F32) == target).astype(F32)
-    w_back = jnp.transpose(w_top).astype(jnp.bfloat16)
-    w_top = w_top.astype(jnp.bfloat16)
+    w_back = thrice(jnp.transpose(w_top))
+    w_near = jnp.concatenate([thrice(for_near == target), thrice(w_top)], axis=0)
+    w_cond = jnp.concatenate([thrice(for_cond == target), thrice(w_top)], axis=0)
+    picked = pick_rows(w_cond, cc[:, 0:8].reshape(128, 128))
+    payload_c, top_cond = picked[: 8 * ngx], picked[8 * ngx :]
     all_in(tops, ngx, gr.at[4])
     top_t = tops[:, 0:16].reshape(128, 128)
     top_c = tops[:, 16:32].reshape(128, 128)
     top_up, top_dn, top_lf, top_rt = conductances(top_c, 8)
-    top_bound = WALL_RATIO * pick_rows(w_top, cond_rows)
+    top_bound = WALL_RATIO * top_cond
     top_inv = 1.0 / (top_up + top_dn + top_lf + top_rt + top_bound)
 
     all_in(nb, ngy, gr.at[2])
-    near_rows = thirds(nb[...].reshape(128, 128))
-    payload = payload_c + pick_rows(w_near, near_rows)
+    picked = pick_rows(w_near, nb[...].reshape(128, 128))
+    payload = payload_c + picked[: 8 * ngx]
     m3s[...] = payload.reshape(ngx, 8, 128)
     spread(lambda k: m3s.at[gxd(k)[0]], m3r, i, ngx, gxd, gs.at[3], gr.at[3])
     m3r[i] = m3s[i]
-    top_src = top_bound * pick_rows(w_top, near_rows)
+    top_src = top_bound * picked[8 * ngx :]
     for _ in range(SWEEPS):
-        top_t = sweep(top_t, top_up, top_dn, top_lf, top_rt, top_src, top_inv)
-    m5s[...] = pick_rows(w_back, thirds(top_t)).reshape(ngy, 8, 128)
+        tiles = top_t.reshape(16, 8, 128)
+        above, below = (pltpu.roll(tiles, n, 1).reshape(128, 128) for n in (1, 7))
+        total = top_up * above + top_dn * below
+        total = total + top_lf * pltpu.roll(top_t, 1, 1) + top_rt * pltpu.roll(top_t, 127, 1)
+        top_t = (total + top_src) * top_inv
+    m5s[...] = pick_rows(w_back, top_t).reshape(ngy, 8, 128)
     spread(lambda k: m5s.at[gyd(k)[1]], m5r, j, ngy, gyd, gs.at[5], gr.at[5])
     m5r[j] = m5s[j]
 
@@ -480,17 +496,28 @@
 
     cool_at = per_block(cool[0:1], cool[1:2])
 
+    def advance_second(x, yt):
+        fluid_ref[x, pl.ds(yt, 8)] = stencil(t1p, x, yt, lambda n: coef[n, x, pl.ds(yt, 8)])
+
+    def second_middle(x, carry):
+        for yt in middle:
+            advance_second(x, yt)
+        return carry
+
+    lax.fori_loop(1, nx - 1, second_middle, 0, unroll=5)
     y1[1]()
     x1[1]()
-
-    def second_body(x, carry):
+    for x in (0, nx - 1):
+        second_middle(x, 0)
+
+    def second_edge(x, carry):
         t1p[x + 1, PAD - 1 : PAD, :] = y1_recv[0, x]
         t1p[x + 1, PAD + ny : PAD + ny + 1, :] = y1_recv[1, x]
-        for yt in range(0, ny, 8):
-            fluid_ref[x, pl.ds(yt, 8)] = stencil(t1p, x, yt, lambda n: coef[n, x, pl.ds(yt, 8)])
+        for yt in (0, ny - 8):
+            advance_second(x, yt)
         return carry
 
-    lax.fori_loop(0, nx, second_body, 0, unroll=4)
+    lax.fori_loop(0, nx, second_edge, 0, unroll=4)
 
     all_in(m3r, ngx, gr.at[3])
     arrived = m3r[0]
@@ -506,7 +533,7 @@
         temps = sweep(temps, c_up, c_dn, c_lf, c_rt, source, inverse)
     solid_ref[...] = temps.reshape(2, layers, width)
 
-    for group in (wy, wx, ys, xt, xk, xu, y1, x1):
+    for group in (wy, wx, ys, yh, xt, xk, xu, y1, x1):
         group[2]()
     for copy, sends, gets in corners:
         pl.when(sends)(copy.wait_send)
@@ -574,6 +601,8 @@
                 pltpu.VMEM((nx, ny, 128), F32),
                 pltpu.VMEM((2, 3, nx, 1, nz), F32),
                 pltpu.VMEM((2, 3, nx, 1, nz), F32),
+                pltpu.VMEM((2, 2, nx, nz), jnp.bfloat16),
+                pltpu.VMEM((2, 2, nx, nz), jnp.bfloat16),
                 pltpu.VMEM((2, nx, 1, nz), F32),
                 pltpu.VMEM((2, nx, 1, nz), F32),
                 pltpu.VMEM((8, cells), F32),
@@ -591,8 +620,8 @@
                 pltpu.VMEM((ngy, 8, 128), F32),
                 pltpu.VMEM((ngy, 8, 128), F32),
                 dma((3, 2)),
-                dma((4, 2)),
-                dma((4, 2)),
+                dma((5, 2)),
+                dma((5, 2)),
                 dma((2, 2)),
                 dma((2, 2)),
                 dma((2, 2)),

time: 29.8 us -> 28.6 us (0.960)
  Pallas kernels: 28.3 us -> 27.1 us
    pallas_call x1, Pallas kernels: 27 us -> 25.8 us  [shards(): pl.pallas_call(functools.partial(kernel, ngx, ngy), out_shape=(pltpu.VMEM...]
where the time goes in v5:
time: 28.6 us; the launch traced here: 28.4 us
  Pallas kernels  27.1 us (95%)
  between operations  1.29 us (5%)
    pallas_call x1, Pallas kernels, shards(): pl.pallas_call(functools.partial(kernel, ngx, ngy), out_shape=(pltpu.VMEM...  25.8 us
    pallas_call x1, Pallas kernels, shards(): pl.pallas_call(finish, out_shape=(jax.ShapeDtypeStruct(temp.shape, F32),...  1.35 us

profile of v5, /device:TPU:1, one launch (start us, length us, event | category | flops | bytes accessed | tf_op | source)
XLA Modules:
  0.0 28.4 jit_solution(13504326524613319730)
XLA Ops:
  1.3 25.8 %coupled_step.1 = (f32[32,32,512]{2,1,0:T(8,128)S(1)}, f32[32,32]{1,0:T(8,128)S(1)}, f32[2,32,128]{2,1,0:T(8,128)S(1)}) custom-call(f32[32,32,512]{2,1,0:T(8,128)} %t_hbm.1, bf16[32,32,512]{2,1,0:T(8,128)(2,1)} %k_hbm.1, bf16[3,32,32,512]{3,2,1,0:T(8,128)(2,1)} %v_hbm.1, f32[32,32]{1,0:T(8,128)} %wall_ref.1, s32[1]{0:T(128)S(6)} %copy.12.count_ref, ...), custom_call_target="tpu_custom_call" | custom-call | tf_op jit(solution)/shard_map/coupled_step/pallas_call | solution.py:582
  27.0 1.4 %write_out.1 = (f32[32,32,512]{2,1,0:T(8,128)}, f32[32,32]{1,0:T(8,128)}, f32[2,32,128]{2,1,0:T(8,128)}) custom-call(f32[32,32,512]{2,1,0:T(8,128)S(1)} %get-tuple-element.6.fluid, f32[32,32]{1,0:T(8,128)S(1)} %get-tuple-element.7.wall, f32[2,32,128]{2,1,0:T(8,128)S(1)} %get-tuple-element.8.solid), custom_call_target="tpu_custom_call" | custom-call | tf_op jit(solution)/shard_map/write_out/pallas_call | solution.py:639
